TPU v7x, 128 devices: a whole 4x4x4 slice. The times are simulated.
128 devices in a mesh: row: 16 (over x, z), col: 8 (over y, core).
Axes of the slice: x: 4, y: 4, z: 4, core: 2. Of those that a mesh axis runs over, the one named last changes fastest.
Arguments:
- depth_old: float32 [384, 256, 256], P(('row', 'col')), may hold values from 0 to 1.2
- flow_x_old: float32 [384, 256, 256], P(('row', 'col')), may hold values from -4 to 4
- flow_y_old: float32 [384, 256, 256], P(('row', 'col')), may hold values from -4 to 4
- floor_old: bfloat16 [384, 256, 256], P(('row', 'col')), may hold values from 0 to 0.29882812
- width_old: bfloat16 [384, 256, 256], P(('row', 'col')), may hold values from 0.5 to 4
- chan_old: bfloat16 [384, 256, 256], P(('row', 'col')), may hold values from 0.5 to 1
- rough_old: bfloat16 [384, 256, 256], P(('row', 'col')), may hold values from 0.019897461 to 0.099609375
- route: int32 [384, 3], replicated, may hold values from 0 to 15, as said below
- wet_tiles: int32 [16, 24], P('row', 'col'), may hold values 0 or 1
Outputs:
- depth_new: float32 [4096, 6144], P('row', 'col')
- flow_x_new: float32 [4096, 6144], P('row', 'col')
- flow_y_new: float32 [4096, 6144], P('row', 'col')
Inputs may be any that keep to these rules, and one draw needn't show every extreme that they name: route is a bijection of old slots onto new slots. Exactly 3 tiles leave each device and 3 arrive; those leaving one device go to distinct mesh rows and distinct mesh columns, and those arriving at one device come from distinct mesh rows and distinct mesh columns.
All inputs are finite; a program needn't handle non-finite values. No bound on the sum of `wet_tiles` on one device may be relied on, other than what follows from the above.
Results may differ from a plain program's by a relative error of at most 0.0003.
Values may be sent and summed in bfloat16 or wider, within the bound.
A program may use at most 128 MiB of HBM per device.

v0:
```python
import jax
import jax.numpy as jnp
from jax import lax
from jax.sharding import PartitionSpec as P

ITERS = 4


GRAV = 9.81
CELL = 5.0
STEP = 0.1
RMIN = 0.1


def extended(block, sides, width):
    for axis, dim in sides:
        count = lax.axis_size(axis)
        forward = [(i, i + 1) for i in range(count - 1)]
        backward = [(target, source) for source, target in forward]
        low = lax.ppermute(
            lax.slice_in_dim(block, block.shape[dim] - width, None, axis=dim), axis, forward
        )
        high = lax.ppermute(lax.slice_in_dim(block, 0, width, axis=dim), axis, backward)
        block = jnp.concatenate([low, block, high], axis=dim)
    return block


def shift_east(values):
    return jnp.pad(values[:, 1:], ((0, 0), (0, 1)))


def shift_west(values):
    return jnp.pad(values[:, :-1], ((0, 0), (1, 0)))


def shift_south(values):
    return jnp.pad(values[1:, :], ((0, 1), (0, 0)))


def shift_north(values):
    return jnp.pad(values[:-1, :], ((1, 0), (0, 0)))


def face_flow(flow, surface, channel_bed, width, chan, rough, wetness, shifter):
    surface_n = shifter(surface)
    bed_n = shifter(channel_bed)
    crest = jnp.maximum(surface, surface_n) - jnp.maximum(channel_bed, bed_n)
    face_width = jnp.minimum(width, shifter(width))
    face_chan = jnp.minimum(chan, shifter(chan))
    flow_area = face_width * crest + (CELL - face_width) * jnp.maximum(crest - face_chan, 0.0)
    face_rough = 0.5 * (rough + shifter(rough))
    radius = jnp.maximum(flow_area / CELL, RMIN)
    slope = (surface_n - surface) / CELL
    updated = (flow - GRAV * STEP * flow_area * slope) / (
        1.0 + GRAV * STEP * face_rough * face_rough * jnp.abs(flow) / (CELL * radius ** (7.0 / 3.0))
    )
    return jnp.where(wetness * shifter(wetness) > 0, updated, 0.0)


def advance(water, along_x, along_y, floor, width, chan, rough, wetness):
    channel_bed = floor - chan
    surface = channel_bed + water
    new_x = face_flow(along_x, surface, channel_bed, width, chan, rough, wetness, shift_east)
    new_y = face_flow(along_y, surface, channel_bed, width, chan, rough, wetness, shift_south)
    volume = CELL * width * jnp.minimum(water, chan) + CELL * CELL * jnp.maximum(water - chan, 0.0)
    inflow = shift_west(new_x) - new_x + shift_north(new_y) - new_y
    volume = jnp.maximum(volume + STEP * inflow, 0.0)
    cap_volume = CELL * width * chan
    water_new = jnp.minimum(volume, cap_volume) / (CELL * width) + jnp.maximum(
        volume - cap_volume, 0.0
    ) / (CELL * CELL)
    return (water_new, new_x, new_y)


def routing(route_grid, own_b, own_a):
    count_b, count_a, slot_count = (route_grid.shape[0], route_grid.shape[1], route_grid.shape[2])
    dest_b = route_grid[..., 0]
    dest_a = route_grid[..., 1]
    dest_slot = route_grid[..., 2]
    index_b = jnp.arange(count_b, dtype=jnp.int32)
    index_a = jnp.arange(count_a, dtype=jnp.int32)
    index_s = jnp.arange(slot_count, dtype=jnp.int32)
    moving = (dest_b != index_b[:, None, None]) | (dest_a != index_a[None, :, None])
    band_move = lax.dynamic_index_in_dim(moving, own_b, 0, keepdims=False)
    band_b = lax.dynamic_index_in_dim(dest_b, own_b, 0, keepdims=False)
    band_a = lax.dynamic_index_in_dim(dest_a, own_b, 0, keepdims=False)
    band_slot = lax.dynamic_index_in_dim(dest_slot, own_b, 0, keepdims=False)
    own_move = lax.dynamic_index_in_dim(band_move, own_a, 0, keepdims=False)
    own_dest_a = lax.dynamic_index_in_dim(band_a, own_a, 0, keepdims=False)
    own_dest_slot = lax.dynamic_index_in_dim(band_slot, own_a, 0, keepdims=False)
    hit_first = own_move[None, :] & (own_dest_a[None, :] == index_a[:, None])
    valid_first = jnp.any(hit_first, 1)
    pick_first = jnp.sum(jnp.where(hit_first, index_s[None, :], 0), 1)
    hit_middle = band_move & (band_a == own_a)
    valid_middle = jnp.any(hit_middle, 1)
    middle_dest = jnp.sum(jnp.where(hit_middle, band_b, 0), 1)
    hit_second = valid_middle[None, :] & (middle_dest[None, :] == index_b[:, None])
    valid_second = jnp.any(hit_second, 1)
    pick_second = jnp.sum(jnp.where(hit_second, index_a[None, :], 0), 1)
    arrive = moving & (dest_b == own_b) & (dest_a == own_a)
    valid_arrive = jnp.any(arrive, (1, 2))
    arrive_slot = jnp.sum(jnp.where(arrive, dest_slot, 0), (1, 2))
    stay_hit = jnp.logical_not(own_move)[None, :] & (own_dest_slot[None, :] == index_s[:, None])
    recv_hit = valid_arrive[None, :] & (arrive_slot[None, :] == index_s[:, None])
    final_index = jnp.sum(jnp.where(stay_hit, index_s[None, :], 0), 1) + jnp.sum(
        jnp.where(recv_hit, slot_count + index_b[None, :], 0), 1
    )
    return (pick_first, valid_first, pick_second, valid_second, final_index)


def pick_tiles(tile_state, tile_shape, picks, valid):
    chosen_state = jnp.where(valid[:, None, None, None], jnp.take(tile_state, picks, axis=0), 0.0)
    chosen_shape = jnp.where(
        valid[:, None, None, None], jnp.take(tile_shape, picks, axis=0), jnp.zeros((), jnp.bfloat16)
    )
    return (chosen_state, chosen_shape)


def across_col(tile_state, tile_shape):
    moved_state = lax.all_to_all(tile_state, "col", split_axis=0, concat_axis=0, tiled=True)
    moved_shape = lax.all_to_all(tile_shape, "col", split_axis=0, concat_axis=0, tiled=True)
    return (moved_state, moved_shape)


def across_row(tile_state, tile_shape):
    moved_state = lax.all_to_all(tile_state, "row", split_axis=0, concat_axis=0, tiled=True)
    moved_shape = lax.all_to_all(tile_shape, "row", split_axis=0, concat_axis=0, tiled=True)
    return (moved_state, moved_shape)


def to_block(tiles, tile_rows, tile_cols):
    fields, tile_side = (tiles.shape[1], tiles.shape[2])
    shaped = tiles.reshape(tile_rows, tile_cols, fields, tile_side, tile_side).transpose(
        2, 0, 3, 1, 4
    )
    return shaped.reshape(fields, tile_rows * tile_side, tile_cols * tile_side)


def body(
    depth_old, flow_x_old, flow_y_old, floor_old, width_old, chan_old, rough_old, route, wet_tiles
):
    mesh_rows = lax.axis_size("row")
    mesh_cols = lax.axis_size("col")
    own_row = lax.axis_index("row")
    own_col = lax.axis_index("col")
    slot_count = depth_old.shape[0]
    tile_side = depth_old.shape[1]
    tile_rows, tile_cols = wet_tiles.shape
    tile_state = jnp.stack([depth_old, flow_x_old, flow_y_old], 1)
    tile_shape = jnp.stack([floor_old, width_old, chan_old, rough_old], 1)
    route_grid = route.reshape(mesh_rows, mesh_cols, slot_count, 3)
    pick_first, valid_first, pick_second, valid_second, final_index = routing(
        route_grid, own_row, own_col
    )
    sent_state, sent_shape = pick_tiles(tile_state, tile_shape, pick_first, valid_first)
    got_state, got_shape = across_col(sent_state, sent_shape)
    sent_state, sent_shape = pick_tiles(got_state, got_shape, pick_second, valid_second)
    got_state, got_shape = across_row(sent_state, sent_shape)
    new_state = jnp.take(jnp.concatenate([tile_state, got_state], 0), final_index, axis=0)
    new_shape = jnp.take(jnp.concatenate([tile_shape, got_shape], 0), final_index, axis=0)
    wet_cells = jnp.repeat(jnp.repeat(wet_tiles, tile_side, 0), tile_side, 1).astype(jnp.bfloat16)
    shape_block = jnp.concatenate([to_block(new_shape, tile_rows, tile_cols), wet_cells[None]], 0)
    rim_width = 1
    shape_ext = extended(shape_block, (("row", 1), ("col", 2)), rim_width).astype(jnp.float32)
    floor = shape_ext[0]
    width_raw = shape_ext[1]
    width = jnp.where(width_raw > 0, width_raw, 1.0)
    chan = shape_ext[2]
    rough = shape_ext[3]
    wetness = shape_ext[4]
    state_block = to_block(new_state, tile_rows, tile_cols)
    for outer in range(ITERS // rim_width):
        state_ext = extended(state_block, (("row", 1), ("col", 2)), rim_width)
        water, along_x, along_y = (state_ext[0], state_ext[1], state_ext[2])
        water, along_x, along_y = advance(
            water, along_x, along_y, floor, width, chan, rough, wetness
        )
        state_block = jnp.stack([water, along_x, along_y], 0)[
            :, rim_width:-rim_width, rim_width:-rim_width
        ]
    return (state_block[0], state_block[1], state_block[2])


def solution(mesh):
    placed = (
        P(("row", "col"), None, None),
        P(("row", "col"), None, None),
        P(("row", "col"), None, None),
        P(("row", "col"), None, None),
        P(("row", "col"), None, None),
        P(("row", "col"), None, None),
        P(("row", "col"), None, None),
        P(),
        P("row", "col"),
    )
    return jax.shard_map(
        body,
        mesh=mesh,
        in_specs=placed,
        out_specs=(P("row", "col"), P("row", "col"), P("row", "col")),
        check_vma=False,
    )
```

profile of v0, /device:TPU:22, one launch (start us, length us, event | category | flops | bytes accessed | tf_op | source)
XLA Modules:
  0.0 731.0 jit_solution(4628394051748094686)
XLA Ops:
  4.8 2.8 gather_fusion
  7.6 4.7 select_select_fusion.3
  12.3 4.9 all-to-all-start
  18.9 3.7 gather_fusion.3
  22.6 6.4 select_select_fusion.2
  29.0 34.9 %all-to-all-done = bf16[8,4,256,256]{3,2,1,0:T(8,128)(2,1)} async-done(((bf16[8,4,256,256]{3,2,1,0:T(8,128)(2,1)}), bf16[8,4,256,256]{3,2,1,0:T(8,128)(2,1)}, u32[]{:S(2)}, u32[]{:S(2)}) %all-to-all-start) | async-done | bytes 4194336 | tf_op jit(solution)/shard_map/all_to_all | solution.py:121
  63.9 7.8 %all-to-all-start.2 = ((f32[8,3,256,256]{3,2,1,0:T(8,128)}), f32[8,3,256,256]{3,2,1,0:T(8,128)}, u32[]{:S(2)}, u32[]{:S(2)}) async-start(f32[8,3,256,256]{3,2,1,0:T(8,128)} %select_select_fusion.2), calls=%async_computation.2 | async-start | bytes 12582912 | tf_op jit(solution)/shard_map/all_to_all | solution.py:120
  72.9 6.8 gather_fusion.1
  79.7 7.6 %select_select_fusion.1 = bf16[16,4,256,256]{3,2,1,0:T(8,128)(2,1)} fusion(bf16[16,4,256,256]{3,2,1,0:T(8,128)(2,1)} %gather_fusion.1, pred[16]{0:T(512)(128)(4,1)S(1)} %compare_and_fusion.1, pred[16]{0:T(512)(128)(4,1)S(1)} %fusion.13), kind=kLoop, calls=%fused_computation.9 | loop fusion | flops 8388608 | bytes 16777248 | tf_op jit(solution)/shard_map/jit(_where)/select_n | solution.py:113
  87.3 53.4 %all-to-all-done.2 = f32[8,3,256,256]{3,2,1,0:T(8,128)} async-done(((f32[8,3,256,256]{3,2,1,0:T(8,128)}), f32[8,3,256,256]{3,2,1,0:T(8,128)}, u32[]{:S(2)}, u32[]{:S(2)}) %all-to-all-start.2) | async-done | bytes 6291488 | tf_op jit(solution)/shard_map/all_to_all | solution.py:120
  140.8 8.3 %all-to-all-start.1 = ((bf16[16,4,256,256]{3,2,1,0:T(8,128)(2,1)}), bf16[16,4,256,256]{3,2,1,0:T(8,128)(2,1)}, u32[]{:S(2)}, u32[]{:S(2)}) async-start(bf16[16,4,256,256]{3,2,1,0:T(8,128)(2,1)} %select_select_fusion.1), calls=%async_computation.1 | async-start | bytes 16777216 | tf_op jit(solution)/shard_map/all_to_all | solution.py:127
  149.0 8.7 %gather_fusion.4 = f32[16,3,256,256]{3,2,1,0:T(8,128)} fusion(f32[8,3,256,256]{3,2,1,0:T(8,128)} %all-to-all-done.2, s32[1024]{0:T(1024)S(1)} %pad_clamp_fusion.1), kind=kCustom, calls=%fused_computation.4 | custom fusion | bytes 25165888 | tf_op jit(solution)/shard_map/jit(_take)/gather | solution.py:112
  157.8 11.7 %select_select_fusion = f32[16,3,256,256]{3,2,1,0:T(8,128)} fusion(f32[16,3,256,256]{3,2,1,0:T(8,128)} %gather_fusion.4, pred[16]{0:T(512)(128)(4,1)S(1)} %compare_and_fusion.1, pred[16]{0:T(512)(128)(4,1)S(1)} %fusion.13), kind=kLoop, calls=%fused_computation.7 | loop fusion | flops 6291456 | bytes 25165856 | tf_op jit(solution)/shard_map/jit(_where)/select_n | solution.py:112
  169.5 123.7 %all-to-all-done.1 = bf16[16,4,256,256]{3,2,1,0:T(8,128)(2,1)} async-done(((bf16[16,4,256,256]{3,2,1,0:T(8,128)(2,1)}), bf16[16,4,256,256]{3,2,1,0:T(8,128)(2,1)}, u32[]{:S(2)}, u32[]{:S(2)}) %all-to-all-start.1) | async-done | bytes 8388640 | tf_op jit(solution)/shard_map/all_to_all | solution.py:127
  293.2 11.6 %all-to-all-start.3 = ((f32[16,3,256,256]{3,2,1,0:T(8,128)}), f32[16,3,256,256]{3,2,1,0:T(8,128)}, u32[]{:S(2)}, u32[]{:S(2)}) async-start(f32[16,3,256,256]{3,2,1,0:T(8,128)} %select_select_fusion), calls=%async_computation.3 | async-start | bytes 25165824 | tf_op jit(solution)/shard_map/all_to_all | solution.py:126
  305.7 10.9 %pad_maximum_fusion.1 = bf16[19,4,256,256]{3,2,1,0:T(8,128)(2,1)} fusion(bf16[16,4,256,256]{3,2,1,0:T(8,128)(2,1)} %all-to-all-done.1, bf16[3,1,256,256]{3,2,1,0:T(8,128)(2,1)S(1)} %bitcast.271, bf16[3,1,256,256]{3,2,1,0:T(8,128)(2,1)S(1)} %bitcast.273, bf16[3,1,256,256]{3,2,1,0:T(8,128)(2,1)S(1)} %bitcast.275, bf16[3,1,256,256]{3,2,1,0:T(8,128)(2,1)S(1)} %bitcast.277), kind=kLoop, calls=%fused_computation.8 | loop fusion | flops 19922944 | bytes 19922944 | tf_op jit(solution)/shard_map/concatenate | solution.py:160
  316.6 4.5 gather_fusion.2
  323.5 5.3 collective-permute-start.1
  329.3 1.9 collective-permute-start
  331.3 193.6 %collective-permute-done.1 = bf16[5,1,768]{2,0,1:T(8,128)(2,1)S(1)} collective-permute-done((bf16[5,1,768]{2,0,1:T(8,128)(2,1)S(1)}, bf16[5,1,768]{2,0,1:T(8,128)(2,1)S(1)}, u32[]{:S(2)}, u32[]{:S(2)}) %collective-permute-start.1) | collective-permute-done | bytes 7712 | tf_op jit(solution)/shard_map/ppermute | solution.py:23
  527.5 1.9 collective-permute-start.3
  529.5 2.4 collective-permute-start.2
  531.9 2.5 collective-permute-done.2
  534.4 6.0 maximum_convert_fusion
  540.4 10.5 %pad_maximum_fusion = f32[19,3,256,256]{3,2,1,0:T(8,128)} fusion(f32[16,3,256,256]{3,2,1,0:T(8,128)} %all-to-all-done.3, f32[3,1,256,256]{3,2,1,0:T(8,128)} %bitcast.264, f32[3,1,256,256]{3,2,1,0:T(8,128)} %bitcast.267, f32[3,1,256,256]{3,2,1,0:T(8,128)} %bitcast.269), kind=kLoop, calls=%fused_computation.6 | loop fusion | flops 11206656 | bytes 29884416 | tf_op jit(solution)/shard_map/concatenate | solution.py:159
  550.9 6.0 gather_fusion.5
  558.6 2.0 copy.72
  563.6 6.6 collective-permute-start.5
  573.1 3.9 slice_bitcast_fusion.16
  579.1 2.1 copy.75
  582.1 1.9 collective-permute-start.7
  584.0 2.5 collective-permute-start.6
  586.6 3.1 slice_bitcast_fusion.12
  594.9 4.1 divide_select_fusion.7
  599.1 4.1 divide_select_fusion.6
  606.1 2.2 copy.78
  608.3 5.0 collective-permute-start.9
  613.3 2.2 copy.77
  620.0 2.1 copy.80
  623.5 2.2 copy.79
  626.7 1.9 collective-permute-start.11
  628.6 2.6 collective-permute-start.10
  631.2 2.3 collective-permute-done.10
  638.4 3.5 divide_select_fusion.5
  641.9 3.2 add_bitcast_fusion.2
  647.0 2.2 copy.82
  649.2 5.3 collective-permute-start.13
  654.5 2.2 copy.81
  661.2 2.1 copy.84
  664.7 2.2 copy.83
  667.9 1.9 collective-permute-start.15
  669.8 2.6 collective-permute-start.14
  672.5 2.3 collective-permute-done.14
  679.7 3.5 divide_select_fusion.3
  683.2 3.2 add_bitcast_fusion.1
  688.2 2.2 copy.86
  690.4 4.7 collective-permute-start.17
  695.1 2.2 copy.85
  701.8 2.1 copy.88
  705.3 2.2 copy.87
  710.4 2.7 collective-permute-start.18
  713.1 2.3 collective-permute-done.18
  720.2 3.5 divide_select_fusion.1
  723.7 2.8 add_bitcast_fusion
  (247 shorter events, 76.4 us)
Async XLA Ops:
  3.1 4.5 copy-start.55
  3.2 4.5 copy-start.57
  12.3 4.9 copy-start.48
  12.3 51.6 %all-to-all-start = ((bf16[8,4,256,256]{3,2,1,0:T(8,128)(2,1)}), bf16[8,4,256,256]{3,2,1,0:T(8,128)(2,1)}, u32[]{:S(2)}, u32[]{:S(2)}) async-start(bf16[8,4,256,256]{3,2,1,0:T(8,128)(2,1)} %select_select_fusion.3), calls=%async_computation | async-start | bytes 8388608 | tf_op jit(solution)/shard_map/all_to_all | solution.py:121
  18.9 3.7 copy-start.56
  18.9 3.7 copy-start.58
  63.9 76.9 %all-to-all-start.2 = ((f32[8,3,256,256]{3,2,1,0:T(8,128)}), f32[8,3,256,256]{3,2,1,0:T(8,128)}, u32[]{:S(2)}, u32[]{:S(2)}) async-start(f32[8,3,256,256]{3,2,1,0:T(8,128)} %select_select_fusion.2), calls=%async_computation.2 | async-start | bytes 12582912 | tf_op jit(solution)/shard_map/all_to_all | solution.py:120
  140.8 152.5 %all-to-all-start.1 = ((bf16[16,4,256,256]{3,2,1,0:T(8,128)(2,1)}), bf16[16,4,256,256]{3,2,1,0:T(8,128)(2,1)}, u32[]{:S(2)}, u32[]{:S(2)}) async-start(bf16[16,4,256,256]{3,2,1,0:T(8,128)(2,1)} %select_select_fusion.1), calls=%async_computation.1 | async-start | bytes 16777216 | tf_op jit(solution)/shard_map/all_to_all | solution.py:127
  169.5 135.4 %copy-start.63 = (s32[1,3]{1,0:T(1,128)S(1)}, s32[1,3]{1,0:T(1,128)}, u32[]{:S(2)}) copy-start(s32[1,3]{1,0:T(1,128)} %param.17) | copy-start | bytes 40
  169.5 135.5 %copy-start.62 = (pred[3]{0:T(512)(128)(4,1)S(1)}, pred[3]{0:T(512)(128)(4,1)}, u32[]{:S(2)}) copy-start(pred[3]{0:T(512)(128)(4,1)} %get-tuple-element.32) | copy-start | bytes 13
  169.5 136.0 %copy-start.59 = (pred[16]{0:T(512)(128)(4,1)S(1)}, pred[16]{0:T(512)(128)(4,1)}, u32[]{:S(2)}) copy-start(pred[16]{0:T(512)(128)(4,1)} %get-tuple-element.29) | copy-start | bytes 52
  169.5 136.2 %copy-start.49 = (bf16[3,256,256]{2,1,0:T(8,128)(2,1)S(1)}, bf16[3,256,256]{2,1,0:T(8,128)(2,1)}, u32[]{:S(2)}) copy-start(bf16[3,256,256]{2,1,0:T(8,128)(2,1)} %param.15) | copy-start | bytes 1179652
  169.5 136.2 %copy-start.50 = (bf16[3,256,256]{2,1,0:T(8,128)(2,1)S(1)}, bf16[3,256,256]{2,1,0:T(8,128)(2,1)}, u32[]{:S(2)}) copy-start(bf16[3,256,256]{2,1,0:T(8,128)(2,1)} %param.14) | copy-start | bytes 1179652
  169.5 136.2 %copy-start.51 = (bf16[3,256,256]{2,1,0:T(8,128)(2,1)S(1)}, bf16[3,256,256]{2,1,0:T(8,128)(2,1)}, u32[]{:S(2)}) copy-start(bf16[3,256,256]{2,1,0:T(8,128)(2,1)} %param.13) | copy-start | bytes 1179652
  169.5 136.2 %copy-start.52 = (bf16[3,256,256]{2,1,0:T(8,128)(2,1)S(1)}, bf16[3,256,256]{2,1,0:T(8,128)(2,1)}, u32[]{:S(2)}) copy-start(bf16[3,256,256]{2,1,0:T(8,128)(2,1)} %param.12) | copy-start | bytes 1179652
  293.2 247.2 %all-to-all-start.3 = ((f32[16,3,256,256]{3,2,1,0:T(8,128)}), f32[16,3,256,256]{3,2,1,0:T(8,128)}, u32[]{:S(2)}, u32[]{:S(2)}) async-start(f32[16,3,256,256]{3,2,1,0:T(8,128)} %select_select_fusion), calls=%async_computation.3 | async-start | bytes 25165824 | tf_op jit(solution)/shard_map/all_to_all | solution.py:126
  305.7 15.4 %copy-start.60 = (pred[3]{0:T(512)(128)(4,1)}, pred[3]{0:T(512)(128)(4,1)S(1)}, u32[]{:S(2)}) copy-start(pred[3]{0:T(512)(128)(4,1)S(1)} %compare_and_fusion.2) | copy-start | bytes 13
  323.5 201.4 %collective-permute-start.1 = (bf16[5,1,768]{2,0,1:T(8,128)(2,1)S(1)}, bf16[5,1,768]{2,0,1:T(8,128)(2,1)S(1)}, u32[]{:S(2)}, u32[]{:S(2)}) collective-permute-start(bf16[5,1,768]{2,0,1:T(8,128)(2,1)S(1)} %copy.69), channel_id=1, source_target_pairs={{8,0},{16,8},{24,16},{32,24},{40,32},{48,40},{56,48},{64,56},{72,6... | collective-permute-start | bytes 23048 | tf_op jit(solution)/shard_map/ppermute | solution.py:23
  329.3 196.1 %collective-permute-start = (bf16[5,1,768]{2,0,1:T(8,128)(2,1)S(1)}, bf16[5,1,768]{2,0,1:T(8,128)(2,1)}, u32[]{:S(2)}, u32[]{:S(2)}) collective-permute-start(bf16[5,1,768]{2,0,1:T(8,128)(2,1)S(1)} %copy.68), channel_id=1, source_target_pairs={{0,8},{8,16},{16,24},{24,32},{32,40},{40,48},{48,56},{56,64},{64,7... | collective-permute-start | bytes 23048 | tf_op jit(solution)/shard_map/ppermute | solution.py:20
  526.7 7.8 %copy-start.38 = (bf16[1,256,768]{1,2,0:T(8,128)(2,1)S(1)}, bf16[1,256,768]{1,2,0:T(8,128)(2,1)}, u32[]{:S(2)}) copy-start(bf16[1,256,768]{1,2,0:T(8,128)(2,1)} %copy-done.37) | copy-start | bytes 1179652
  527.5 4.3 collective-permute-start.3
  529.5 5.0 collective-permute-start.2
  550.9 6.0 copy-start.61
  563.6 13.4 %collective-permute-start.5 = (f32[3,1,768]{2,1,0:T(1,128)S(1)}, f32[3,1,768]{2,1,0:T(1,128)}, u32[]{:S(2)}, u32[]{:S(2)}) collective-permute-start(f32[3,1,768]{2,1,0:T(1,128)S(1)} %copy.74), channel_id=1, source_target_pairs={{8,0},{16,8},{24,16},{32,24},{40,32},{48,40},{56,48},{64,56},{72,6... | collective-permute-start | bytes 27656 | tf_op jit(solution)/shard_map/ppermute | solution.py:23
  571.2 8.0 %collective-permute-start.4 = (f32[3,1,768]{2,1,0:T(1,128)}, f32[3,1,768]{2,1,0:T(1,128)}, u32[]{:S(2)}, u32[]{:S(2)}) collective-permute-start(f32[3,1,768]{2,1,0:T(1,128)} %copy.73), channel_id=1, source_target_pairs={{0,8},{8,16},{16,24},{24,32},{32,40},{40,48},{48,56},{56,64},{64,7... | collective-permute-start | bytes 27656 | tf_op jit(solution)/shard_map/ppermute | solution.py:20
  582.1 9.0 %collective-permute-start.7 = (f32[3,258,1]{1,2,0:T(1,128)S(1)}, f32[3,258,1]{1,2,0:T(1,128)S(1)}, u32[]{:S(2)}, u32[]{:S(2)}) collective-permute-start(f32[3,258,1]{1,2,0:T(1,128)S(1)} %get-tuple-element.54), channel_id=1, source_target_pairs={{1,0},{2,1},{3,2},{4,3},{5,4},{6,5},{7,6},{9,8},{10,9},{11,10},{12... | collective-permute-start | bytes 9296 | tf_op jit(solution)/shard_map/ppermute | solution.py:23
  584.0 5.6 copy-start.47
  584.0 7.0 collective-permute-start.6
  586.6 3.2 copy-start.46
  589.8 2.9 slice-start
  591.0 2.2 slice-start.1
  608.3 11.7 %collective-permute-start.9 = (f32[3,1,768]{2,1,0:T(1,128)}, f32[3,1,768]{2,1,0:T(1,128)}, u32[]{:S(2)}, u32[]{:S(2)}) collective-permute-start(f32[3,1,768]{2,1,0:T(1,128)} %copy.78), channel_id=1, source_target_pairs={{8,0},{16,8},{24,16},{32,24},{40,32},{48,40},{56,48},{64,56},{72,6... | collective-permute-start | bytes 27656 | tf_op jit(solution)/shard_map/ppermute | solution.py:23
  615.5 8.0 %collective-permute-start.8 = (f32[3,1,768]{2,1,0:T(1,128)}, f32[3,1,768]{2,1,0:T(1,128)}, u32[]{:S(2)}, u32[]{:S(2)}) collective-permute-start(f32[3,1,768]{2,1,0:T(1,128)} %copy.77), channel_id=1, source_target_pairs={{0,8},{8,16},{16,24},{24,32},{32,40},{40,48},{48,56},{56,64},{64,7... | collective-permute-start | bytes 27656 | tf_op jit(solution)/shard_map/ppermute | solution.py:20
  625.7 7.9 %copy-start.31 = (f32[3,1,768]{1,2,0:T(8,128)S(1)}, f32[3,1,768]{1,2,0:T(8,128)}, u32[]{:S(2)}) copy-start(f32[3,1,768]{1,2,0:T(8,128)} %copy.80) | copy-start | bytes 27652
  625.7 7.9 %copy-start.34 = (f32[3,1,768]{1,2,0:T(8,128)S(1)}, f32[3,1,768]{1,2,0:T(8,128)}, u32[]{:S(2)}) copy-start(f32[3,1,768]{1,2,0:T(8,128)} %copy.79) | copy-start | bytes 27652
  626.7 4.5 collective-permute-start.11
  628.6 4.9 collective-permute-start.10
  633.6 2.1 copy-start.42
  635.2 2.2 copy-start.9
  635.2 2.6 copy-start.12
  635.3 2.8 copy-start.3
  635.3 3.2 copy-start.6
  641.9 3.2 copy-start.1
  649.2 12.0 %collective-permute-start.13 = (f32[3,1,768]{2,1,0:T(1,128)}, f32[3,1,768]{2,1,0:T(1,128)}, u32[]{:S(2)}, u32[]{:S(2)}) collective-permute-start(f32[3,1,768]{2,1,0:T(1,128)} %copy.82), channel_id=1, source_target_pairs={{8,0},{16,8},{24,16},{32,24},{40,32},{48,40},{56,48},{64,56},{72,6... | collective-permute-start | bytes 27656 | tf_op jit(solution)/shard_map/ppermute | solution.py:23
  656.8 8.0 %collective-permute-start.12 = (f32[3,1,768]{2,1,0:T(1,128)}, f32[3,1,768]{2,1,0:T(1,128)}, u32[]{:S(2)}, u32[]{:S(2)}) collective-permute-start(f32[3,1,768]{2,1,0:T(1,128)} %copy.81), channel_id=1, source_target_pairs={{0,8},{8,16},{16,24},{24,32},{32,40},{40,48},{48,56},{56,64},{64,7... | collective-permute-start | bytes 27656 | tf_op jit(solution)/shard_map/ppermute | solution.py:20
  666.9 7.9 %copy-start.32 = (f32[3,1,768]{1,2,0:T(8,128)S(1)}, f32[3,1,768]{1,2,0:T(8,128)}, u32[]{:S(2)}) copy-start(f32[3,1,768]{1,2,0:T(8,128)} %copy.84) | copy-start | bytes 27652
  666.9 7.9 %copy-start.35 = (f32[3,1,768]{1,2,0:T(8,128)S(1)}, f32[3,1,768]{1,2,0:T(8,128)}, u32[]{:S(2)}) copy-start(f32[3,1,768]{1,2,0:T(8,128)} %copy.83) | copy-start | bytes 27652
  667.9 4.6 collective-permute-start.15
  669.8 4.9 collective-permute-start.14
  676.4 2.2 copy-start.10
  676.4 2.6 copy-start.13
  676.5 2.8 copy-start.4
  676.5 3.2 copy-start.7
  683.2 3.2 copy-start.2
  690.4 11.4 %collective-permute-start.17 = (f32[3,1,768]{2,1,0:T(1,128)}, f32[3,1,768]{2,1,0:T(1,128)}, u32[]{:S(2)}, u32[]{:S(2)}) collective-permute-start(f32[3,1,768]{2,1,0:T(1,128)} %copy.86), channel_id=1, source_target_pairs={{8,0},{16,8},{24,16},{32,24},{40,32},{48,40},{56,48},{64,56},{72,6... | collective-permute-start | bytes 27656 | tf_op jit(solution)/shard_map/ppermute | solution.py:23
  697.3 8.0 %collective-permute-start.16 = (f32[3,1,768]{2,1,0:T(1,128)}, f32[3,1,768]{2,1,0:T(1,128)}, u32[]{:S(2)}, u32[]{:S(2)}) collective-permute-start(f32[3,1,768]{2,1,0:T(1,128)} %copy.85), channel_id=1, source_target_pairs={{0,8},{8,16},{16,24},{24,32},{32,40},{40,48},{48,56},{56,64},{64,7... | collective-permute-start | bytes 27656 | tf_op jit(solution)/shard_map/ppermute | solution.py:20
  707.5 7.9 %copy-start.33 = (f32[3,1,768]{1,2,0:T(8,128)S(1)}, f32[3,1,768]{1,2,0:T(8,128)}, u32[]{:S(2)}) copy-start(f32[3,1,768]{1,2,0:T(8,128)} %copy.88) | copy-start | bytes 27652
  707.5 7.9 %copy-start.36 = (f32[3,1,768]{1,2,0:T(8,128)S(1)}, f32[3,1,768]{1,2,0:T(8,128)}, u32[]{:S(2)}) copy-start(f32[3,1,768]{1,2,0:T(8,128)} %copy.87) | copy-start | bytes 27652
  708.5 4.6 collective-permute-start.19
  710.4 4.9 collective-permute-start.18
  716.9 2.2 copy-start.11
  716.9 2.6 copy-start.14
  717.0 2.9 copy-start.5
  717.0 3.2 copy-start.8
  (26 other events, 44.1 us)
where the time goes:
time: 742 us; the launch traced here: 731 us
  waiting for transfers between devices  420 us (57%)
  other arithmetic  117 us (16%)
  local copies, waits for them, and re-layouts  101 us (14%)
  starting transfers between devices  91.5 us (12%)
    ppermute x10, waiting for transfers between devices, extended(): lax.ppermute(lax.slice_in_dim(block, 0, width, axis=dim), axis, backward)  194 us
    all_to_all x1, waiting for transfers between devices, across_row(): lax.all_to_all(tile_shape, 'row', split_axis=0, concat_axis=0, tiled=True)  124 us
    all_to_all x1, waiting for transfers between devices, across_col(): lax.all_to_all(tile_state, 'col', split_axis=0, concat_axis=0, tiled=True)  53.4 us
    ppermute x10, starting transfers between devices, extended(): lax.ppermute(lax.slice_in_dim(block, 0, width, axis=dim), axis, backward)  36.5 us
    all_to_all x1, waiting for transfers between devices, across_col(): lax.all_to_all(tile_shape, 'col', split_axis=0, concat_axis=0, tiled=True)  34.9 us
    ppermute x10, starting transfers between devices, extended(): lax.ppermute(lax.slice_in_dim(block, block.shape[dim] - width, None, axis...  22.4 us
    select_n x5, other arithmetic, face_flow(): return jnp.where(wetness * shifter(wetness) > 0, updated, 0.0)  18.6 us
    select_n x2, other arithmetic, pick_tiles(): jnp.where(valid[:, None, None, None], jnp.take(tile_state, picks, axis=0)...  18.1 us
  transfers between devices with their start and end apart: 24, of which 12 were waited for; matrix products, arithmetic and copies ran while one was open for 14% of the time, Pallas kernels for 0%

commit v1 on v0

v1 whole, which is shorter than its diff:
```python
import jax
import jax.numpy as jnp
from jax import lax
from jax.experimental import pallas as pl
from jax.experimental.pallas import tpu as pltpu
from jax.sharding import PartitionSpec as P

ITERS = 4
GRAV = 9.81
CELL = 5.0
STEP = 0.1
RMIN = 0.1

NX, NZ, NC = 4, 4, 8
DEVICES = NX * NZ * NC
SLOTS = 3
HALVES = 2
CHUNKS = SLOTS * HALVES
TILE = 256
BLOCK = 16
LANES = 128
FIRST = ("yxz", "xzy", "zyx") * 2
SECOND = ("zxy", "yzx", "xyz") * 2
PIECES = (CHUNKS, NX, NZ, NC, BLOCK, LANES)

PAD = 8
ROWS = TILE + 2 * PAD
COLS = SLOTS * TILE
WIDE = COLS + LANES
STRIPS = ROWS // 8
REACH = 4
FIELDS = 7
WATER, FLOW_X, FLOW_Y, BED, WIDTH, CHAN, ROUGH = range(FIELDS)
F32 = jnp.float32


def to_code(values):
    return values.astype(jnp.int32).astype(jnp.int16)


def flow_code(flow):
    root = jnp.sqrt(jnp.sqrt(jnp.abs(flow) * 0.25))
    size = jnp.minimum(root * 32767.0 + 0.5, 32767.0).astype(jnp.int32)
    return jnp.where(flow < 0, -size, size).astype(jnp.int16)


def flow_value(code):
    return (code * code) * (code * jnp.abs(code)) * (4.0 / 32767.0**4)


def floor_code(floor):
    coarse = (floor * 65536.0).astype(jnp.int32)
    fine = -((floor * 16777216.0 + 0.5).astype(jnp.int32))
    return jnp.where(floor < 2.0**-9, fine, coarse).astype(jnp.int16)


def floor_value(code):
    return jnp.where(code < 0, code * -(2.0**-24), code * 2.0**-16)


def part(ref, chunk, axis, index):
    if axis == "x":
        return ref.at[chunk, index]
    if axis == "z":
        return ref.at[chunk, :, index]
    return ref.at[chunk, :, :, index]


def migrate_and_route(
    depth_ref, fx_ref, fy_ref, floor_ref, width_ref, chan_ref, rough_ref, source_ref, wet_ref,
    water_out, fx_out, fy_out,
    coded, first_a, first_b, middle, sorted_, second_a, second_b, arrived,
    fields, sent_w, sent_e, got_e, got_w, level, volume, cap, inverse,
    bed_x, wide_x, deep_x, drag_x, bed_y, wide_y, deep_y, drag_y,
    send_sem, recv_sem, local_sem, rim_send, rim_recv,
):
    row = lax.axis_index("row")
    col = lax.axis_index("col")
    own_x = row // NZ
    own_z = row % NZ

    def place(x, z, c):
        return (x * NZ + z, c)

    west = (row, (col + NC - 1) % NC)
    east = (row, (col + 1) % NC)
    north = ((row + NX * NZ - 1) % (NX * NZ), col)
    south = ((row + 1) % (NX * NZ), col)

    barrier = pltpu.get_barrier_semaphore()
    greeted = [place((own_x + d) % NX, own_z, col) for d in (1, 2, 3)]
    greeted += [place(own_x, (own_z + d) % NZ, col) for d in (1, 2, 3)]
    greeted += [place(own_x, own_z, (col + d) % NC) for d in range(1, NC)]
    greeted += [north, south]
    for device in greeted:
        pl.semaphore_signal(barrier, inc=1, device_id=device, device_id_type=pl.DeviceIdType.MESH)

    def encode(chunk):
        slot, half = chunk // HALVES, chunk % HALVES
        lanes = pl.ds(half * LANES, LANES)

        def block(b, _):
            rows = pl.ds(pl.multiple_of(b * BLOCK, BLOCK), BLOCK)

            def put(plane, code):
                coded[chunk, b // NZ, b % NZ, plane] = code

            depth = depth_ref[slot, rows, lanes] * 16384.0
            high = depth.astype(jnp.int32)
            low = ((depth - high.astype(F32)) * 65536.0).astype(jnp.int32) - 32768
            put(0, high.astype(jnp.int16))
            put(1, low.astype(jnp.int16))
            put(2, flow_code(fx_ref[slot, rows, lanes]))
            put(3, flow_code(fy_ref[slot, rows, lanes]))
            put(4, floor_code(floor_ref[slot, rows, lanes].astype(F32)))
            put(5, to_code(width_ref[slot, rows, lanes].astype(F32) * 256.0))
            put(6, to_code(chan_ref[slot, rows, lanes].astype(F32) * 256.0))
            put(7, to_code(rough_ref[slot, rows, lanes].astype(F32) * 8192.0))
            return 0

        lax.fori_loop(0, TILE // BLOCK, block, 0)

    def decode(chunk):
        slot, half = chunk // HALVES, chunk % HALVES
        lanes = pl.ds(slot * TILE + half * LANES, LANES)
        wet = wet_ref[0, slot].astype(F32)

        def block(b, _):
            rows = pl.ds(pl.multiple_of(PAD + b * BLOCK, 8), BLOCK)

            def get(plane):
                return arrived[chunk, b // NZ, b % NZ, plane].astype(jnp.int32).astype(F32)

            chan = get(6) * (1.0 / 256.0)
            fields[WATER, rows, lanes] = get(0) * 2.0**-14 + (get(1) + 32768.0) * 2.0**-30
            fields[FLOW_X, rows, lanes] = flow_value(get(2))
            fields[FLOW_Y, rows, lanes] = flow_value(get(3))
            fields[BED, rows, lanes] = floor_value(get(4)) - chan
            fields[WIDTH, rows, lanes] = get(5) * (1.0 / 256.0)
            fields[CHAN, rows, lanes] = chan
            fields[ROUGH, rows, lanes] = get(7) * (1.0 / 8192.0) * wet - (1.0 - wet)
            return 0

        lax.fori_loop(0, TILE // BLOCK, block, 0)

    def copies(stage, chunk, axis, source, target):
        base = (stage * CHUNKS + chunk) * 8
        remote = []
        if axis == "y":
            me = col
            steps = [4, 5, 2, 3, 6, 7, 1]
            partners = [((col + (d // 2) * 2) % NC) // 2 * 2 + (col + d % 2) % 2 for d in steps]
            devices = [place(own_x, own_z, c) for c in partners]
        elif axis == "x":
            me = own_x
            partners = [(own_x + d) % NX for d in (2, 1, 3)]
            devices = [place(x, own_z, col) for x in partners]
        else:
            me = own_z
            partners = [(own_z + d) % NZ for d in (2, 1, 3)]
            devices = [place(own_x, z, col) for z in partners]
        for q, (partner, device) in enumerate(zip(partners, devices)):
            remote.append(
                pltpu.make_async_remote_copy(
                    src_ref=part(source, chunk, axis, partner),
                    dst_ref=part(target, chunk, axis, me),
                    send_sem=send_sem.at[base + q],
                    recv_sem=recv_sem.at[base + q],
                    device_id=device,
                    device_id_type=pl.DeviceIdType.MESH,
                )
            )
        local = pltpu.make_async_copy(
            part(source, chunk, axis, me),
            part(target, chunk, axis, me),
            local_sem.at[stage * CHUNKS + chunk],
        )
        return remote, local

    started = []

    def launch(stage, chunk, axis, source, target):
        remote, local = copies(stage, chunk, axis, source, target)
        for copy in remote:
            copy.start()
        local.start()
        started.extend(remote)
        return remote, local

    def landed(pair):
        remote, local = pair
        for copy in remote:
            copy.wait_recv()
        local.wait()

    encode(0)
    pl.semaphore_wait(barrier, len(greeted))
    flying = []
    for chunk in range(CHUNKS):
        if chunk > 0:
            encode(chunk)
        flying.append(launch(0, chunk, FIRST[chunk][0], coded, first_a))
    for stage, source, target in ((1, first_a, first_b), (2, first_b, middle)):
        for chunk in range(CHUNKS):
            landed(flying[chunk])
            flying[chunk] = launch(stage, chunk, FIRST[chunk][stage], source, target)
    for chunk in range(CHUNKS):
        landed(flying[chunk])

    taken = middle.reshape(CHUNKS * DEVICES, BLOCK, LANES)
    ordered = sorted_.reshape(CHUNKS * DEVICES, BLOCK, LANES)
    for chunk in range(CHUNKS):
        slot, half = chunk // HALVES, chunk % HALVES

        def move(k, _):
            for u in range(8):
                d = k * 8 + u
                ordered[chunk * DEVICES + d] = taken[source_ref[slot * DEVICES + d] + half * DEVICES]
            return 0

        lax.fori_loop(0, DEVICES // 8, move, 0)
        flying[chunk] = launch(3, chunk, SECOND[chunk][0], sorted_, second_a)
    for stage, source, target in ((4, second_a, second_b), (5, second_b, arrived)):
        for chunk in range(CHUNKS):
            landed(flying[chunk])
            flying[chunk] = launch(stage, chunk, SECOND[chunk][stage - 3], source, target)
    for chunk in range(CHUNKS):
        landed(flying[chunk])
        decode(chunk)

    lane = lax.broadcasted_iota(jnp.int32, (8, LANES), 1)

    def pack(k, _):
        rows = pl.ds(pl.multiple_of(PAD + k * 8, 8), 8)
        left = jnp.zeros((8, LANES), F32)
        right = jnp.zeros((8, LANES), F32)
        for f in range(FIELDS):
            here = (lane >= REACH * f) & (lane < REACH * (f + 1))
            low = fields[f, rows, pl.ds(0, LANES)]
            high = fields[f, rows, pl.ds(COLS - LANES, LANES)]
            left = jnp.where(here, pltpu.roll(low, REACH * f, 1) if f else low, left)
            right = jnp.where(here, pltpu.roll(high, REACH * (f + 1), 1), right)
        out = pl.ds(pl.multiple_of(k * 8, 8), 8)
        sent_w[out, :] = left
        sent_e[out, :] = right
        return 0

    lax.fori_loop(0, TILE // 8, pack, 0)

    def rim(number, source, target, device):
        copy = pltpu.make_async_remote_copy(
            src_ref=source, dst_ref=target, send_sem=rim_send.at[number],
            recv_sem=rim_recv.at[number], device_id=device,
            device_id_type=pl.DeviceIdType.MESH,
        )
        copy.start()
        started.append(copy)
        return copy

    side = [rim(0, sent_w, got_e, west), rim(1, sent_e, got_w, east)]
    for copy in side:
        copy.wait_recv()

    at_east = col == NC - 1
    at_west = col == 0

    def unpack(k, _):
        source = pl.ds(pl.multiple_of(k * 8, 8), 8)
        rows = pl.ds(pl.multiple_of(PAD + k * 8, 8), 8)
        from_e = got_e[source, :]
        from_w = got_w[source, :]
        for f in range(FIELDS):
            low = pltpu.roll(from_e, LANES - REACH * f, 1) if f else from_e
            high = pltpu.roll(from_w, LANES - REACH * (f + 1), 1)
            if f == ROUGH:
                low = jnp.where(at_east, -1.0, low)
                high = jnp.where(at_west, -1.0, high)
            fill = 1.0 if f in (WIDTH, CHAN) else (-1.0 if f == ROUGH else 0.0)
            mixed = jnp.where(lane < REACH, low, jnp.where(lane >= LANES - REACH, high, fill))
            fields[f, rows, pl.ds(COLS, LANES)] = mixed
        return 0

    lax.fori_loop(0, TILE // 8, unpack, 0)

    ends = [
        rim(2, fields.at[:, pl.ds(PAD, 8), :], fields.at[:, pl.ds(PAD + TILE, 8), :], north),
        rim(3, fields.at[:, pl.ds(TILE, 8), :], fields.at[:, pl.ds(0, 8), :], south),
    ]
    for copy in ends:
        copy.wait_recv()
    for copy in started:
        copy.wait_send()
    first = fields[ROUGH, pl.ds(0, 8), :]
    fields[ROUGH, pl.ds(0, 8), :] = jnp.where(row == 0, -1.0, first)
    last = fields[ROUGH, pl.ds(PAD + TILE, 8), :]
    fields[ROUGH, pl.ds(PAD + TILE, 8), :] = jnp.where(row == NX * NZ - 1, -1.0, last)

    bottom = lax.broadcasted_iota(jnp.int32, (8, WIDE), 0) == 7
    top = lax.broadcasted_iota(jnp.int32, (8, WIDE), 0) == 0

    def strip(k):
        return pl.ds(pl.multiple_of(k * 8, 8), 8)

    def to_east(values):
        return pltpu.roll(values, WIDE - 1, 1)

    def to_west(values):
        return pltpu.roll(values, 1, 1)

    def to_south(values, after):
        return jnp.where(bottom, pltpu.roll(after, 7, 0), pltpu.roll(values, 7, 0))

    def faces(k, _):
        here = strip(k)
        there = strip(jnp.minimum(k + 1, STRIPS - 1))
        water = fields[WATER, here, :]
        bed, width = fields[BED, here, :], fields[WIDTH, here, :]
        chan, rough = fields[CHAN, here, :], fields[ROUGH, here, :]
        level[here, :] = bed + water
        volume[here, :] = CELL * width * jnp.minimum(water, chan) + CELL * CELL * jnp.maximum(
            water - chan, 0.0
        )
        cap[here, :] = CELL * width * chan
        inverse[here, :] = 1.0 / (CELL * width)
        for shift, bed_f, wide_f, deep_f, drag_f in (
            (lambda f, v: to_east(v), bed_x, wide_x, deep_x, drag_x),
            (lambda f, v: to_south(v, fields[f, there, :]), bed_y, wide_y, deep_y, drag_y),
        ):
            bed_f[here, :] = jnp.maximum(bed, shift(BED, bed))
            wide_f[here, :] = jnp.minimum(width, shift(WIDTH, width))
            deep_f[here, :] = jnp.minimum(chan, shift(CHAN, chan))
            rough_n = shift(ROUGH, rough)
            mean = 0.5 * (rough + rough_n)
            drag_f[here, :] = jnp.where(
                jnp.minimum(rough, rough_n) > 0, (GRAV * STEP / CELL) * mean * mean, -1.0
            )
        return 0

    lax.fori_loop(0, STRIPS, faces, 0)

    def face_flow(flow, surface, surface_n, bed_f, wide_f, deep_f, drag_f):
        crest = jnp.maximum(surface, surface_n) - bed_f
        area = wide_f * crest + (CELL - wide_f) * jnp.maximum(crest - deep_f, 0.0)
        radius = jnp.maximum(area * (1.0 / CELL), RMIN)
        friction = drag_f * jnp.abs(flow) * jnp.exp(jnp.log(radius) * (-7.0 / 3.0))
        updated = (flow - (GRAV * STEP / CELL) * area * (surface_n - surface)) / (1.0 + friction)
        return jnp.where(drag_f > 0, updated, 0.0)

    for step in range(ITERS):
        final = step == ITERS - 1

        def sweep(k, above):
            here = strip(k)
            there = strip(jnp.minimum(k + 1, STRIPS - 1))
            surface = level[here, :]
            surface_s = to_south(surface, level[there, :])
            new_x = face_flow(
                fields[FLOW_X, here, :], surface, to_east(surface),
                bed_x[here, :], wide_x[here, :], deep_x[here, :], drag_x[here, :],
            )
            new_y = face_flow(
                fields[FLOW_Y, here, :], surface, surface_s,
                bed_y[here, :], wide_y[here, :], deep_y[here, :], drag_y[here, :],
            )
            rolled = pltpu.roll(new_y, 1, 0)
            inflow = to_west(new_x) - new_x + jnp.where(top, above, rolled) - new_y
            held = jnp.maximum(volume[here, :] + STEP * inflow, 0.0)
            most = cap[here, :]
            water = jnp.minimum(held, most) * inverse[here, :] + jnp.maximum(
                held - most, 0.0
            ) * (1.0 / (CELL * CELL))
            if final:
                out = strip(jnp.clip(k - PAD // 8, 0, TILE // 8 - 1))
                water_out[out, :] = water[:, :COLS]
                fx_out[out, :] = new_x[:, :COLS]
                fy_out[out, :] = new_y[:, :COLS]
            else:
                fields[FLOW_X, here, :] = new_x
                fields[FLOW_Y, here, :] = new_y
                volume[here, :] = held
                level[here, :] = fields[BED, here, :] + water
            return rolled

        stop = (PAD + TILE) // 8 if final else STRIPS
        lax.fori_loop(0, stop, sweep, jnp.zeros((8, WIDE), F32))


def body(depth, flow_x, flow_y, floor, width, chan, rough, route, wet_tiles):
    target = (route[:, 0] * NC + route[:, 1]) * SLOTS + route[:, 2]
    old = jnp.arange(DEVICES * SLOTS, dtype=jnp.int32)
    where_held = (old % SLOTS) * (HALVES * DEVICES) + old // SLOTS
    slot_major = (old % DEVICES) * SLOTS + old // DEVICES
    source = jnp.sum(
        jnp.where(slot_major[:, None] == target[None, :], where_held[None, :], 0), axis=1
    )
    vmem = pl.BlockSpec(memory_space=pltpu.VMEM)
    smem = pl.BlockSpec(memory_space=pltpu.SMEM)
    pieces = pltpu.VMEM(PIECES, jnp.int16)
    grid = pltpu.VMEM((ROWS, WIDE), F32)
    edge = pltpu.VMEM((TILE, LANES), F32)
    out = jax.ShapeDtypeStruct((TILE, COLS), F32)
    return pl.pallas_call(
        migrate_and_route,
        out_shape=(out, out, out),
        in_specs=[vmem] * 7 + [smem] * 2,
        out_specs=(vmem, vmem, vmem),
        scratch_shapes=[pieces] * 8
        + [pltpu.VMEM((FIELDS, ROWS, WIDE), F32)]
        + [edge] * 4
        + [grid] * 12
        + [
            pltpu.SemaphoreType.DMA((6 * CHUNKS * 8,)),
            pltpu.SemaphoreType.DMA((6 * CHUNKS * 8,)),
            pltpu.SemaphoreType.DMA((6 * CHUNKS,)),
            pltpu.SemaphoreType.DMA((4,)),
            pltpu.SemaphoreType.DMA((4,)),
        ],
        compiler_params=pltpu.CompilerParams(
            collective_id=0, has_side_effects=True, vmem_limit_bytes=58 * 2**20
        ),
    )(depth, flow_x, flow_y, floor, width, chan, rough, source, wet_tiles)


def solution(mesh):
    tiles = P(("row", "col"), None, None)
    block = P("row", "col")
    return jax.shard_map(
        body,
        mesh=mesh,
        in_specs=(tiles,) * 7 + (P(), block),
        out_specs=(block, block, block),
        check_vma=False,
    )
```

time: 742 us -> 144 us (0.19)
  the two profiles are of different devices: /device:TPU:22 before, /device:TPU:1 now
where the time goes in v1:
time: 144 us
  Pallas kernels  137 us (95%)
  local copies, waits for them, and re-layouts  4.44 us (3%)
  other arithmetic  1.65 us (1%)
    pallas_call x1, Pallas kernels, body(): pl.pallas_call(migrate_and_route, out_shape=(out, out, out), in_specs=[vm...  137 us
    unnamed x7, local copies, waits for them, and re-layouts  4.44 us

profile of v1, /device:TPU:1, one launch (start us, length us, event | category | flops | bytes accessed | tf_op | source)
XLA Modules:
  0.0 143.9 jit_solution(9189812109950798503)
XLA Ops:
  0.6 0.8 add_reduce_fusion
  1.5 0.8 select_reduce_fusion.source_ref
  2.3 137.1 %shard_map.112 = (f32[256,768]{1,0:T(8,128)}, f32[256,768]{1,0:T(8,128)}, f32[256,768]{1,0:T(8,128)}) custom-call(f32[3,256,256]{2,1,0:T(8,128)} %depth_ref.1, f32[3,256,256]{2,1,0:T(8,128)} %fx_ref.1, f32[3,256,256]{2,1,0:T(8,128)} %fy_ref.1, bf16[3,256,256]{2,1,0:T(8,128)(2,1)} %floor_ref.1, bf16[3,256,256]{2,1,0:T(8,128)(2,1)} %width_ref.1, ...), custom_call_target="tpu_custom_call" | custom-call | tf_op jit(solution)/shard_map/pallas_call | solution.py:402
  139.4 0.0 copy-start.1
  139.4 2.1 %copy.15 = f32[256,768]{1,0:T(8,128)} copy(f32[256,768]{1,0:T(8,128)} %get-tuple-element.8) | data formatting | bytes 1572864
  141.6 0.0 copy-done.1
  141.6 0.0 copy-start
  141.6 0.9 copy.16
  142.4 0.5 copy-done
  143.0 0.9 copy.17
  (1 shorter events, 0.0 us)
Async XLA Ops:
  139.4 2.1 %copy-start.1 = (f32[256,768]{1,0:T(8,128)S(1)}, f32[256,768]{1,0:T(8,128)}, u32[]{:S(2)}) copy-start(f32[256,768]{1,0:T(8,128)} %get-tuple-element.9) | copy-start | bytes 2359300
  141.6 1.4 copy-start

commit v2 on v1

--- a/solution.py
+++ b/solution.py
@@ -30,6 +30,9 @@
 STRIPS = ROWS // 8
 REACH = 4
 FIELDS = 7
+BLOCKS = WIDE // LANES
+PARTS = 4
+LOG2_E = 1.4426950408889634
 WATER, FLOW_X, FLOW_Y, BED, WIDTH, CHAN, ROUGH = range(FIELDS)
 F32 = jnp.float32
 
@@ -67,12 +70,14 @@
 
 
 def migrate_and_route(
-    depth_ref, fx_ref, fy_ref, floor_ref, width_ref, chan_ref, rough_ref, source_ref, wet_ref,
+    depth_hbm, fx_hbm, fy_hbm, floor_hbm, width_hbm, chan_hbm, rough_hbm, source_ref, wet_ref,
+    water_hbm, fx_out_hbm, fy_out_hbm,
+    depth_ref, fx_ref, fy_ref, floor_ref, width_ref, chan_ref, rough_ref,
     water_out, fx_out, fy_out,
-    coded, first_a, first_b, middle, sorted_, second_a, second_b, arrived,
-    fields, sent_w, sent_e, got_e, got_w, level, volume, cap, inverse,
-    bed_x, wide_x, deep_x, drag_x, bed_y, wide_y, deep_y, drag_y,
-    send_sem, recv_sem, local_sem, rim_send, rim_recv,
+    coded, first_a, first_b, middle, second_a, second_b, arrived,
+    fields, sent_w, sent_e, got_e, got_w, level, volume, cap, inverse, flow_x, flow_y,
+    bed_x, part_x, deep_x, drag_x, gate_x, bed_y, part_y, deep_y, drag_y, gate_y,
+    send_sem, recv_sem, local_sem, rim_send, rim_recv, in_sem, out_sem,
 ):
     row = lax.axis_index("row")
     col = lax.axis_index("col")
@@ -86,6 +91,20 @@
     east = (row, (col + 1) % NC)
     north = ((row + NX * NZ - 1) % (NX * NZ), col)
     south = ((row + 1) % (NX * NZ), col)
+
+    loads = []
+    for slot in range(SLOTS):
+        pairs = (
+            (depth_hbm, depth_ref), (fx_hbm, fx_ref), (fy_hbm, fy_ref), (floor_hbm, floor_ref),
+            (width_hbm, width_ref), (chan_hbm, chan_ref), (rough_hbm, rough_ref),
+        )
+        group = [
+            pltpu.make_async_copy(hbm.at[slot], ref.at[slot], in_sem.at[slot * FIELDS + n])
+            for n, (hbm, ref) in enumerate(pairs)
+        ]
+        for copy in group:
+            copy.start()
+        loads.append(group)
 
     barrier = pltpu.get_barrier_semaphore()
     greeted = [place((own_x + d) % NX, own_z, col) for d in (1, 2, 3)]
@@ -98,6 +117,9 @@
     def encode(chunk):
         slot, half = chunk // HALVES, chunk % HALVES
         lanes = pl.ds(half * LANES, LANES)
+        if half == 0:
+            for copy in loads[slot]:
+                copy.wait()
 
         def block(b, _):
             rows = pl.ds(pl.multiple_of(b * BLOCK, BLOCK), BLOCK)
@@ -207,8 +229,11 @@
     for chunk in range(CHUNKS):
         landed(flying[chunk])
 
+    for copy in started:
+        copy.wait_send()
+    started.clear()
     taken = middle.reshape(CHUNKS * DEVICES, BLOCK, LANES)
-    ordered = sorted_.reshape(CHUNKS * DEVICES, BLOCK, LANES)
+    ordered = coded.reshape(CHUNKS * DEVICES, BLOCK, LANES)
     for chunk in range(CHUNKS):
         slot, half = chunk // HALVES, chunk % HALVES
 
@@ -219,7 +244,7 @@
             return 0
 
         lax.fori_loop(0, DEVICES // 8, move, 0)
-        flying[chunk] = launch(3, chunk, SECOND[chunk][0], sorted_, second_a)
+        flying[chunk] = launch(3, chunk, SECOND[chunk][0], coded, second_a)
     for stage, source, target in ((4, second_a, second_b), (5, second_b, arrived)):
         for chunk in range(CHUNKS):
             landed(flying[chunk])
@@ -258,9 +283,72 @@
         return copy
 
     side = [rim(0, sent_w, got_e, west), rim(1, sent_e, got_w, east)]
+    inner = pl.ds(0, COLS)
+    outer = pl.ds(COLS, LANES)
+    ends = [
+        rim(2, fields.at[:, pl.ds(PAD, 8), inner], fields.at[:, pl.ds(PAD + TILE, 8), inner], north),
+        rim(3, fields.at[:, pl.ds(TILE, 8), inner], fields.at[:, pl.ds(0, 8), inner], south),
+    ]
+
+    row_of = lax.broadcasted_iota(jnp.int32, (8, LANES), 0)
+    bottom = row_of == 7
+    top = row_of == 0
+    right_end = lane == LANES - 1
+    left_end = lane == 0
+
+    def strip(k):
+        return pl.ds(pl.multiple_of(k * 8, 8), 8)
+
+    def block(c):
+        return pl.ds((c % BLOCKS) * LANES, LANES)
+
+    def faces(k, c):
+        here = strip(k)
+        there = strip(jnp.minimum(k + 1, STRIPS - 1))
+        water = fields[WATER, here, block(c)]
+        bed, width = fields[BED, here, block(c)], fields[WIDTH, here, block(c)]
+        chan, rough = fields[CHAN, here, block(c)], fields[ROUGH, here, block(c)]
+        level[here, block(c)] = bed + water
+        volume[here, block(c)] = CELL * width * jnp.minimum(water, chan) + CELL * CELL * (
+            jnp.maximum(water - chan, 0.0)
+        )
+        cap[here, block(c)] = CELL * width * chan
+        inverse[here, block(c)] = 1.0 / (CELL * width) - 1.0 / (CELL * CELL)
+
+        def to_east(f, v):
+            after = pltpu.roll(fields[f, here, block(c + 1)], LANES - 1, 1)
+            return jnp.where(right_end, after, pltpu.roll(v, LANES - 1, 1))
+
+        def to_south(f, v):
+            after = pltpu.roll(fields[f, there, block(c)], 7, 0)
+            return jnp.where(bottom, after, pltpu.roll(v, 7, 0))
+
+        for shift, bed_f, part_f, deep_f, drag_f, gate_f, f, flow in (
+            (to_east, bed_x, part_x, deep_x, drag_x, gate_x, FLOW_X, flow_x),
+            (to_south, bed_y, part_y, deep_y, drag_y, gate_y, FLOW_Y, flow_y),
+        ):
+            bed_f[here, block(c)] = jnp.maximum(bed, shift(BED, bed))
+            part_f[here, block(c)] = 1.0 - jnp.minimum(width, shift(WIDTH, width)) * (1.0 / CELL)
+            deep_f[here, block(c)] = jnp.minimum(chan, shift(CHAN, chan))
+            rough_n = shift(ROUGH, rough)
+            mean = 0.5 * (rough + rough_n)
+            wet = jnp.minimum(rough, rough_n) > 0
+            drag_f[here, block(c)] = jnp.where(wet, (GRAV * STEP / CELL) * mean * mean, 0.0)
+            gate_f[here, block(c)] = jnp.where(wet, GRAV * STEP, 0.0)
+            flow[here, block(c)] = jnp.where(wet, fields[f, here, block(c)], 0.0)
+
+    def many_faces(start, stop, blocks):
+        def one(k, _):
+            for c in blocks:
+                faces(k, c)
+            return 0
+
+        lax.fori_loop(start, stop, one, 0)
+
+    many_faces(1, STRIPS - 2, range(BLOCKS - 2))
+
     for copy in side:
         copy.wait_recv()
-
     at_east = col == NC - 1
     at_west = col == 0
 
@@ -277,112 +365,110 @@
                 high = jnp.where(at_west, -1.0, high)
             fill = 1.0 if f in (WIDTH, CHAN) else (-1.0 if f == ROUGH else 0.0)
             mixed = jnp.where(lane < REACH, low, jnp.where(lane >= LANES - REACH, high, fill))
-            fields[f, rows, pl.ds(COLS, LANES)] = mixed
+            fields[f, rows, outer] = mixed
         return 0
 
     lax.fori_loop(0, TILE // 8, unpack, 0)
-
-    ends = [
-        rim(2, fields.at[:, pl.ds(PAD, 8), :], fields.at[:, pl.ds(PAD + TILE, 8), :], north),
-        rim(3, fields.at[:, pl.ds(TILE, 8), :], fields.at[:, pl.ds(0, 8), :], south),
+    ends += [
+        rim(4, fields.at[:, pl.ds(PAD, 8), outer], fields.at[:, pl.ds(PAD + TILE, 8), outer], north),
+        rim(5, fields.at[:, pl.ds(TILE, 8), outer], fields.at[:, pl.ds(0, 8), outer], south),
     ]
+    many_faces(1, STRIPS - 2, range(BLOCKS - 2, BLOCKS))
     for copy in ends:
         copy.wait_recv()
-    for copy in started:
-        copy.wait_send()
     first = fields[ROUGH, pl.ds(0, 8), :]
     fields[ROUGH, pl.ds(0, 8), :] = jnp.where(row == 0, -1.0, first)
     last = fields[ROUGH, pl.ds(PAD + TILE, 8), :]
     fields[ROUGH, pl.ds(PAD + TILE, 8), :] = jnp.where(row == NX * NZ - 1, -1.0, last)
-
-    bottom = lax.broadcasted_iota(jnp.int32, (8, WIDE), 0) == 7
-    top = lax.broadcasted_iota(jnp.int32, (8, WIDE), 0) == 0
-
-    def strip(k):
-        return pl.ds(pl.multiple_of(k * 8, 8), 8)
-
-    def to_east(values):
-        return pltpu.roll(values, WIDE - 1, 1)
-
-    def to_west(values):
-        return pltpu.roll(values, 1, 1)
-
-    def to_south(values, after):
-        return jnp.where(bottom, pltpu.roll(after, 7, 0), pltpu.roll(values, 7, 0))
-
-    def faces(k, _):
-        here = strip(k)
-        there = strip(jnp.minimum(k + 1, STRIPS - 1))
-        water = fields[WATER, here, :]
-        bed, width = fields[BED, here, :], fields[WIDTH, here, :]
-        chan, rough = fields[CHAN, here, :], fields[ROUGH, here, :]
-        level[here, :] = bed + water
-        volume[here, :] = CELL * width * jnp.minimum(water, chan) + CELL * CELL * jnp.maximum(
-            water - chan, 0.0
-        )
-        cap[here, :] = CELL * width * chan
-        inverse[here, :] = 1.0 / (CELL * width)
-        for shift, bed_f, wide_f, deep_f, drag_f in (
-            (lambda f, v: to_east(v), bed_x, wide_x, deep_x, drag_x),
-            (lambda f, v: to_south(v, fields[f, there, :]), bed_y, wide_y, deep_y, drag_y),
-        ):
-            bed_f[here, :] = jnp.maximum(bed, shift(BED, bed))
-            wide_f[here, :] = jnp.minimum(width, shift(WIDTH, width))
-            deep_f[here, :] = jnp.minimum(chan, shift(CHAN, chan))
-            rough_n = shift(ROUGH, rough)
-            mean = 0.5 * (rough + rough_n)
-            drag_f[here, :] = jnp.where(
-                jnp.minimum(rough, rough_n) > 0, (GRAV * STEP / CELL) * mean * mean, -1.0
-            )
-        return 0
-
-    lax.fori_loop(0, STRIPS, faces, 0)
-
-    def face_flow(flow, surface, surface_n, bed_f, wide_f, deep_f, drag_f):
+    many_faces(0, 1, range(BLOCKS))
+    many_faces(STRIPS - 2, STRIPS, range(BLOCKS))
+
+    def face_flow(flow, surface, surface_n, bed_f, part_f, deep_f, drag_f, gate_f):
         crest = jnp.maximum(surface, surface_n) - bed_f
-        area = wide_f * crest + (CELL - wide_f) * jnp.maximum(crest - deep_f, 0.0)
-        radius = jnp.maximum(area * (1.0 / CELL), RMIN)
-        friction = drag_f * jnp.abs(flow) * jnp.exp(jnp.log(radius) * (-7.0 / 3.0))
-        updated = (flow - (GRAV * STEP / CELL) * area * (surface_n - surface)) / (1.0 + friction)
-        return jnp.where(drag_f > 0, updated, 0.0)
-
+        depth = crest - part_f * jnp.minimum(crest, deep_f)
+        power = jnp.exp2(jnp.log(jnp.maximum(depth, RMIN)) * (-7.0 / 3.0 * LOG2_E))
+        below = 1.0 + drag_f * jnp.abs(flow) * power
+        guess = pl.reciprocal(below, approx=True)
+        guess = guess * (2.0 - below * guess)
+        return (flow - gate_f * depth * (surface_n - surface)) * guess
+
+    every = range(BLOCKS)
     for step in range(ITERS):
         final = step == ITERS - 1
 
-        def sweep(k, above):
+        def sweep(k, carry):
+            rolled, above = carry
             here = strip(k)
             there = strip(jnp.minimum(k + 1, STRIPS - 1))
-            surface = level[here, :]
-            surface_s = to_south(surface, level[there, :])
-            new_x = face_flow(
-                fields[FLOW_X, here, :], surface, to_east(surface),
-                bed_x[here, :], wide_x[here, :], deep_x[here, :], drag_x[here, :],
-            )
-            new_y = face_flow(
-                fields[FLOW_Y, here, :], surface, surface_s,
-                bed_y[here, :], wide_y[here, :], deep_y[here, :], drag_y[here, :],
-            )
-            rolled = pltpu.roll(new_y, 1, 0)
-            inflow = to_west(new_x) - new_x + jnp.where(top, above, rolled) - new_y
-            held = jnp.maximum(volume[here, :] + STEP * inflow, 0.0)
-            most = cap[here, :]
-            water = jnp.minimum(held, most) * inverse[here, :] + jnp.maximum(
-                held - most, 0.0
-            ) * (1.0 / (CELL * CELL))
-            if final:
-                out = strip(jnp.clip(k - PAD // 8, 0, TILE // 8 - 1))
-                water_out[out, :] = water[:, :COLS]
-                fx_out[out, :] = new_x[:, :COLS]
-                fy_out[out, :] = new_y[:, :COLS]
-            else:
-                fields[FLOW_X, here, :] = new_x
-                fields[FLOW_Y, here, :] = new_y
-                volume[here, :] = held
-                level[here, :] = fields[BED, here, :] + water
-            return rolled
-
-        stop = (PAD + TILE) // 8 if final else STRIPS
-        lax.fori_loop(0, stop, sweep, jnp.zeros((8, WIDE), F32))
+            surface = [level[here, block(c)] for c in every]
+            turned = [pltpu.roll(v, LANES - 1, 1) for v in surface]
+            ahead = [pltpu.roll(level[there, block(c)], 7, 0) for c in every]
+            new_x, new_y = [], []
+            for c in every:
+                b = block(c)
+                surface_e = jnp.where(right_end, turned[(c + 1) % BLOCKS], turned[c])
+                surface_s = jnp.where(bottom, ahead[c], rolled[c])
+                new_x.append(
+                    face_flow(
+                        flow_x[here, b], surface[c], surface_e, bed_x[here, b], part_x[here, b],
+                        deep_x[here, b], drag_x[here, b], gate_x[here, b],
+                    )
+                )
+                new_y.append(
+                    face_flow(
+                        flow_y[here, b], surface[c], surface_s, bed_y[here, b], part_y[here, b],
+                        deep_y[here, b], drag_y[here, b], gate_y[here, b],
+                    )
+                )
+            sunk = [pltpu.roll(v, 1, 0) for v in new_y]
+            passed = [pltpu.roll(v, 1, 1) for v in new_x]
+            for c in every:
+                b = block(c)
+                if final and c == BLOCKS - 1:
+                    continue
+                from_w = jnp.where(left_end, passed[c - 1], passed[c])
+                from_n = jnp.where(top, above[c], sunk[c])
+                inflow = from_w - new_x[c] + from_n - new_y[c]
+                held = jnp.maximum(volume[here, b] + STEP * inflow, 0.0)
+                water = jnp.minimum(held, cap[here, b]) * inverse[here, b] + held * (
+                    1.0 / (CELL * CELL)
+                )
+                if final:
+                    out = strip(jnp.maximum(k - PAD // 8, 0))
+                    water_out[out, b] = water
+                    fx_out[out, b] = new_x[c]
+                    fy_out[out, b] = new_y[c]
+                else:
+                    flow_x[here, b] = new_x[c]
+                    flow_y[here, b] = new_y[c]
+                    volume[here, b] = held
+                    level[here, b] = fields[BED, here, b] + water
+            return tuple(ahead), tuple(sunk)
+
+        carry = (
+            tuple(pltpu.roll(level[pl.ds(0, 8), block(c)], 7, 0) for c in every),
+            tuple(jnp.zeros((8, LANES), F32) for c in every),
+        )
+        if not final:
+            lax.fori_loop(0, STRIPS, sweep, carry)
+
+    stores = []
+    begin = 0
+    for piece in range(PARTS):
+        end = PAD // 8 + (piece + 1) * (TILE // 8 // PARTS)
+        carry = lax.fori_loop(begin, end, sweep, carry)
+        begin = end
+        rows = pl.ds(piece * (TILE // PARTS), TILE // PARTS)
+        for n, (ref, hbm) in enumerate(
+            ((water_out, water_hbm), (fx_out, fx_out_hbm), (fy_out, fy_out_hbm))
+        ):
+            copy = pltpu.make_async_copy(ref.at[rows], hbm.at[rows], out_sem.at[piece * 3 + n])
+            copy.start()
+            stores.append(copy)
+    for copy in stores:
+        copy.wait()
+    for copy in started:
+        copy.wait_send()
 
 
 def body(depth, flow_x, flow_y, floor, width, chan, rough, route, wet_tiles):
@@ -393,32 +479,37 @@
     source = jnp.sum(
         jnp.where(slot_major[:, None] == target[None, :], where_held[None, :], 0), axis=1
     )
-    vmem = pl.BlockSpec(memory_space=pltpu.VMEM)
+    whole = pl.BlockSpec(memory_space=pl.ANY)
     smem = pl.BlockSpec(memory_space=pltpu.SMEM)
     pieces = pltpu.VMEM(PIECES, jnp.int16)
     grid = pltpu.VMEM((ROWS, WIDE), F32)
     edge = pltpu.VMEM((TILE, LANES), F32)
     out = jax.ShapeDtypeStruct((TILE, COLS), F32)
+    operands = (depth, flow_x, flow_y, floor, width, chan, rough)
     return pl.pallas_call(
         migrate_and_route,
         out_shape=(out, out, out),
-        in_specs=[vmem] * 7 + [smem] * 2,
-        out_specs=(vmem, vmem, vmem),
-        scratch_shapes=[pieces] * 8
+        in_specs=[whole] * 7 + [smem] * 2,
+        out_specs=(whole, whole, whole),
+        scratch_shapes=[pltpu.VMEM(a.shape, a.dtype) for a in operands]
+        + [pltpu.VMEM((TILE, COLS), F32)] * 3
+        + [pieces] * 7
         + [pltpu.VMEM((FIELDS, ROWS, WIDE), F32)]
         + [edge] * 4
-        + [grid] * 12
+        + [grid] * 16
         + [
             pltpu.SemaphoreType.DMA((6 * CHUNKS * 8,)),
             pltpu.SemaphoreType.DMA((6 * CHUNKS * 8,)),
             pltpu.SemaphoreType.DMA((6 * CHUNKS,)),
-            pltpu.SemaphoreType.DMA((4,)),
-            pltpu.SemaphoreType.DMA((4,)),
+            pltpu.SemaphoreType.DMA((6,)),
+            pltpu.SemaphoreType.DMA((6,)),
+            pltpu.SemaphoreType.DMA((SLOTS * FIELDS,)),
+            pltpu.SemaphoreType.DMA((PARTS * 3,)),
         ],
         compiler_params=pltpu.CompilerParams(
             collective_id=0, has_side_effects=True, vmem_limit_bytes=58 * 2**20
         ),
-    )(depth, flow_x, flow_y, floor, width, chan, rough, source, wet_tiles)
+    )(*operands, source, wet_tiles)
 
 
 def solution(mesh):

time: 144 us -> 137 us (0.951)
  Pallas kernels: 137 us -> 130 us
    pallas_call x1, Pallas kernels: 137 us -> 130 us  [body(): pl.pallas_call(migrate_and_route, out_shape=(out, out, out), in_specs=[wh...]
where the time goes in v2:
time: 137 us
  Pallas kernels  130 us (95%)
  local copies, waits for them, and re-layouts  4.44 us (3%)
  other arithmetic  1.65 us (1%)
    pallas_call x1, Pallas kernels, body(): pl.pallas_call(migrate_and_route, out_shape=(out, out, out), in_specs=[wh...  130 us
    unnamed x7, local copies, waits for them, and re-layouts  4.44 us

profile of v2, /device:TPU:1, one launch (start us, length us, event | category | flops | bytes accessed | tf_op | source)
XLA Modules:
  0.0 136.8 jit_solution(7719248794666727571)
XLA Ops:
  0.6 0.8 add_reduce_fusion
  1.5 0.8 select_reduce_fusion.source_ref
  2.3 130.1 %shard_map.112 = (f32[256,768]{1,0:T(8,128)}, f32[256,768]{1,0:T(8,128)}, f32[256,768]{1,0:T(8,128)}) custom-call(f32[3,256,256]{2,1,0:T(8,128)} %depth_hbm.1, f32[3,256,256]{2,1,0:T(8,128)} %fx_hbm.1, f32[3,256,256]{2,1,0:T(8,128)} %fy_hbm.1, bf16[3,256,256]{2,1,0:T(8,128)(2,1)} %floor_hbm.1, bf16[3,256,256]{2,1,0:T(8,128)(2,1)} %width_hbm.1, ...), custom_call_target="tpu_custom_call" | custom-call | tf_op jit(solution)/shard_map/pallas_call | solution.py:489
  132.4 0.0 copy-start.1
  132.4 2.1 %copy.15 = f32[256,768]{1,0:T(8,128)} copy(f32[256,768]{1,0:T(8,128)} %get-tuple-element.8) | data formatting | bytes 1572864
  134.5 0.0 copy-done.1
  134.5 0.0 copy-start
  134.5 0.9 copy.16
  135.4 0.5 copy-done
  135.9 0.9 copy.17
  (1 shorter events, 0.0 us)
Async XLA Ops:
  132.4 2.1 %copy-start.1 = (f32[256,768]{1,0:T(8,128)S(1)}, f32[256,768]{1,0:T(8,128)}, u32[]{:S(2)}) copy-start(f32[256,768]{1,0:T(8,128)} %get-tuple-element.9) | copy-start | bytes 2359300
  134.5 1.4 %copy-start = (f32[256,768]{1,0:T(8,128)S(1)}, f32[256,768]{1,0:T(8,128)}, u32[]{:S(2)}) copy-start(f32[256,768]{1,0:T(8,128)} %get-tuple-element.10) | copy-start | bytes 2359300

commit v3 on v2

--- a/solution.py
+++ b/solution.py
@@ -24,14 +24,18 @@
 PIECES = (CHUNKS, NX, NZ, NC, BLOCK, LANES)
 
 PAD = 8
-ROWS = TILE + 2 * PAD
+HIGH = 72
+STRIPS = -(-(TILE + 2 * PAD) // HIGH)
+ROWS = STRIPS * HIGH
+EDGE = 1
+SAFE = (TILE + PAD - 1) // HIGH
 COLS = SLOTS * TILE
 WIDE = COLS + LANES
-STRIPS = ROWS // 8
 REACH = 4
 FIELDS = 7
 BLOCKS = WIDE // LANES
 PARTS = 4
+TALL = 64
 LOG2_E = 1.4426950408889634
 WATER, FLOW_X, FLOW_Y, BED, WIDTH, CHAN, ROUGH = range(FIELDS)
 F32 = jnp.float32
@@ -253,24 +257,24 @@
         landed(flying[chunk])
         decode(chunk)
 
-    lane = lax.broadcasted_iota(jnp.int32, (8, LANES), 1)
+    lane = lax.broadcasted_iota(jnp.int32, (TALL, LANES), 1)
 
     def pack(k, _):
-        rows = pl.ds(pl.multiple_of(PAD + k * 8, 8), 8)
-        left = jnp.zeros((8, LANES), F32)
-        right = jnp.zeros((8, LANES), F32)
+        rows = pl.ds(pl.multiple_of(PAD + k * TALL, 8), TALL)
+        left = jnp.zeros((TALL, LANES), F32)
+        right = jnp.zeros((TALL, LANES), F32)
         for f in range(FIELDS):
             here = (lane >= REACH * f) & (lane < REACH * (f + 1))
             low = fields[f, rows, pl.ds(0, LANES)]
             high = fields[f, rows, pl.ds(COLS - LANES, LANES)]
             left = jnp.where(here, pltpu.roll(low, REACH * f, 1) if f else low, left)
             right = jnp.where(here, pltpu.roll(high, REACH * (f + 1), 1), right)
-        out = pl.ds(pl.multiple_of(k * 8, 8), 8)
+        out = pl.ds(pl.multiple_of(k * TALL, 8), TALL)
         sent_w[out, :] = left
         sent_e[out, :] = right
         return 0
 
-    lax.fori_loop(0, TILE // 8, pack, 0)
+    lax.fori_loop(0, TILE // TALL, pack, 0)
 
     def rim(number, source, target, device):
         copy = pltpu.make_async_remote_copy(
@@ -293,18 +297,32 @@
     row_of = lax.broadcasted_iota(jnp.int32, (8, LANES), 0)
     bottom = row_of == 7
     top = row_of == 0
-    right_end = lane == LANES - 1
-    left_end = lane == 0
+    lanes_high = lax.broadcasted_iota(jnp.int32, (HIGH, LANES), 1)
+    right_end = lanes_high == LANES - 1
+    left_end = lanes_high == 0
 
     def strip(k):
-        return pl.ds(pl.multiple_of(k * 8, 8), 8)
+        return pl.ds(pl.multiple_of(k * HIGH, 8), HIGH)
+
+    def below_strip(k):
+        return pl.ds(pl.multiple_of(jnp.minimum((k + 1) * HIGH, ROWS - 8), 8), 8)
+
+    def from_south(values, after):
+        moved = pltpu.roll(values, HIGH - 1, 0)
+        end = jnp.where(bottom, pltpu.roll(after, 7, 0), moved[HIGH - 8 :])
+        return jnp.concatenate([moved[: HIGH - 8], end], 0) if HIGH > 8 else end
+
+    def from_north(values, before):
+        moved = pltpu.roll(values, 1, 0)
+        start = jnp.where(top, before, moved[:8])
+        return (jnp.concatenate([start, moved[8:]], 0) if HIGH > 8 else start), moved[:8]
 
     def block(c):
         return pl.ds((c % BLOCKS) * LANES, LANES)
 
     def faces(k, c):
         here = strip(k)
-        there = strip(jnp.minimum(k + 1, STRIPS - 1))
+        there = below_strip(k)
         water = fields[WATER, here, block(c)]
         bed, width = fields[BED, here, block(c)], fields[WIDTH, here, block(c)]
         chan, rough = fields[CHAN, here, block(c)], fields[ROUGH, here, block(c)]
@@ -320,8 +338,7 @@
             return jnp.where(right_end, after, pltpu.roll(v, LANES - 1, 1))
 
         def to_south(f, v):
-            after = pltpu.roll(fields[f, there, block(c)], 7, 0)
-            return jnp.where(bottom, after, pltpu.roll(v, 7, 0))
+            return from_south(v, fields[f, there, block(c)])
 
         for shift, bed_f, part_f, deep_f, drag_f, gate_f, f, flow in (
             (to_east, bed_x, part_x, deep_x, drag_x, gate_x, FLOW_X, flow_x),
@@ -345,7 +362,7 @@
 
         lax.fori_loop(start, stop, one, 0)
 
-    many_faces(1, STRIPS - 2, range(BLOCKS - 2))
+    many_faces(EDGE, SAFE, range(BLOCKS - 2))
 
     for copy in side:
         copy.wait_recv()
@@ -353,8 +370,8 @@
     at_west = col == 0
 
     def unpack(k, _):
-        source = pl.ds(pl.multiple_of(k * 8, 8), 8)
-        rows = pl.ds(pl.multiple_of(PAD + k * 8, 8), 8)
+        source = pl.ds(pl.multiple_of(k * TALL, 8), TALL)
+        rows = pl.ds(pl.multiple_of(PAD + k * TALL, 8), TALL)
         from_e = got_e[source, :]
         from_w = got_w[source, :]
         for f in range(FIELDS):
@@ -368,20 +385,20 @@
             fields[f, rows, outer] = mixed
         return 0
 
-    lax.fori_loop(0, TILE // 8, unpack, 0)
+    lax.fori_loop(0, TILE // TALL, unpack, 0)
     ends += [
         rim(4, fields.at[:, pl.ds(PAD, 8), outer], fields.at[:, pl.ds(PAD + TILE, 8), outer], north),
         rim(5, fields.at[:, pl.ds(TILE, 8), outer], fields.at[:, pl.ds(0, 8), outer], south),
     ]
-    many_faces(1, STRIPS - 2, range(BLOCKS - 2, BLOCKS))
+    many_faces(EDGE, SAFE, range(BLOCKS - 2, BLOCKS))
     for copy in ends:
         copy.wait_recv()
     first = fields[ROUGH, pl.ds(0, 8), :]
     fields[ROUGH, pl.ds(0, 8), :] = jnp.where(row == 0, -1.0, first)
     last = fields[ROUGH, pl.ds(PAD + TILE, 8), :]
     fields[ROUGH, pl.ds(PAD + TILE, 8), :] = jnp.where(row == NX * NZ - 1, -1.0, last)
-    many_faces(0, 1, range(BLOCKS))
-    many_faces(STRIPS - 2, STRIPS, range(BLOCKS))
+    many_faces(0, EDGE, range(BLOCKS))
+    many_faces(SAFE, STRIPS, range(BLOCKS))
 
     def face_flow(flow, surface, surface_n, bed_f, part_f, deep_f, drag_f, gate_f):
         crest = jnp.maximum(surface, surface_n) - bed_f
@@ -396,75 +413,71 @@
     for step in range(ITERS):
         final = step == ITERS - 1
 
-        def sweep(k, carry):
-            rolled, above = carry
+        def sweep(k, above):
             here = strip(k)
-            there = strip(jnp.minimum(k + 1, STRIPS - 1))
+            there = below_strip(k)
             surface = [level[here, block(c)] for c in every]
             turned = [pltpu.roll(v, LANES - 1, 1) for v in surface]
-            ahead = [pltpu.roll(level[there, block(c)], 7, 0) for c in every]
-            new_x, new_y = [], []
+            new_x = []
             for c in every:
                 b = block(c)
                 surface_e = jnp.where(right_end, turned[(c + 1) % BLOCKS], turned[c])
-                surface_s = jnp.where(bottom, ahead[c], rolled[c])
                 new_x.append(
                     face_flow(
                         flow_x[here, b], surface[c], surface_e, bed_x[here, b], part_x[here, b],
                         deep_x[here, b], drag_x[here, b], gate_x[here, b],
                     )
                 )
-                new_y.append(
-                    face_flow(
-                        flow_y[here, b], surface[c], surface_s, bed_y[here, b], part_y[here, b],
-                        deep_y[here, b], drag_y[here, b], gate_y[here, b],
-                    )
-                )
-            sunk = [pltpu.roll(v, 1, 0) for v in new_y]
             passed = [pltpu.roll(v, 1, 1) for v in new_x]
+            sunk = []
             for c in every:
                 b = block(c)
-                if final and c == BLOCKS - 1:
-                    continue
+                surface_s = from_south(surface[c], level[there, b])
+                new_y = face_flow(
+                    flow_y[here, b], surface[c], surface_s, bed_y[here, b], part_y[here, b],
+                    deep_y[here, b], drag_y[here, b], gate_y[here, b],
+                )
+                from_n, end = from_north(new_y, above[c])
+                sunk.append(end)
                 from_w = jnp.where(left_end, passed[c - 1], passed[c])
-                from_n = jnp.where(top, above[c], sunk[c])
-                inflow = from_w - new_x[c] + from_n - new_y[c]
+                inflow = from_w - new_x[c] + from_n - new_y
                 held = jnp.maximum(volume[here, b] + STEP * inflow, 0.0)
                 water = jnp.minimum(held, cap[here, b]) * inverse[here, b] + held * (
                     1.0 / (CELL * CELL)
                 )
-                if final:
-                    out = strip(jnp.maximum(k - PAD // 8, 0))
-                    water_out[out, b] = water
-                    fx_out[out, b] = new_x[c]
-                    fy_out[out, b] = new_y[c]
-                else:
+                if not final:
                     flow_x[here, b] = new_x[c]
-                    flow_y[here, b] = new_y[c]
+                    flow_y[here, b] = new_y
                     volume[here, b] = held
                     level[here, b] = fields[BED, here, b] + water
-            return tuple(ahead), tuple(sunk)
-
-        carry = (
-            tuple(pltpu.roll(level[pl.ds(0, 8), block(c)], 7, 0) for c in every),
-            tuple(jnp.zeros((8, LANES), F32) for c in every),
-        )
+                elif c < BLOCKS - 1:
+                    water_out[here, b] = water
+                    fx_out[here, b] = new_x[c]
+                    fy_out[here, b] = new_y
+            return tuple(sunk)
+
+        carry = tuple(jnp.zeros((8, LANES), F32) for c in every)
         if not final:
             lax.fori_loop(0, STRIPS, sweep, carry)
 
     stores = []
     begin = 0
+    sent = 0
     for piece in range(PARTS):
-        end = PAD // 8 + (piece + 1) * (TILE // 8 // PARTS)
+        end = -(-(PAD + (piece + 1) * (TILE // PARTS)) // HIGH)
         carry = lax.fori_loop(begin, end, sweep, carry)
         begin = end
-        rows = pl.ds(piece * (TILE // PARTS), TILE // PARTS)
+        until = min(TILE, end * HIGH - PAD) if piece < PARTS - 1 else TILE
+        size = until - sent
         for n, (ref, hbm) in enumerate(
             ((water_out, water_hbm), (fx_out, fx_out_hbm), (fy_out, fy_out_hbm))
         ):
-            copy = pltpu.make_async_copy(ref.at[rows], hbm.at[rows], out_sem.at[piece * 3 + n])
+            copy = pltpu.make_async_copy(
+                ref.at[pl.ds(PAD + sent, size)], hbm.at[pl.ds(sent, size)], out_sem.at[piece * 3 + n]
+            )
             copy.start()
             stores.append(copy)
+        sent = until
     for copy in stores:
         copy.wait()
     for copy in started:
@@ -492,7 +505,7 @@
         in_specs=[whole] * 7 + [smem] * 2,
         out_specs=(whole, whole, whole),
         scratch_shapes=[pltpu.VMEM(a.shape, a.dtype) for a in operands]
-        + [pltpu.VMEM((TILE, COLS), F32)] * 3
+        + [pltpu.VMEM((ROWS, COLS), F32)] * 3
         + [pieces] * 7
         + [pltpu.VMEM((FIELDS, ROWS, WIDE), F32)]
         + [edge] * 4

time: 137 us -> 117 us (0.85)
  Pallas kernels: 130 us -> 110 us
    pallas_call x1, Pallas kernels: 130 us -> 110 us  [body(): pl.pallas_call(migrate_and_route, out_shape=(out, out, out), in_specs=[wh...]
where the time goes in v3:
time: 117 us
  Pallas kernels  110 us (94%)
  local copies, waits for them, and re-layouts  4.44 us (4%)
  other arithmetic  1.65 us (1%)
    pallas_call x1, Pallas kernels, body(): pl.pallas_call(migrate_and_route, out_shape=(out, out, out), in_specs=[wh...  110 us
    unnamed x7, local copies, waits for them, and re-layouts  4.44 us

profile of v3, /device:TPU:1, one launch (start us, length us, event | category | flops | bytes accessed | tf_op | source)
XLA Modules:
  0.0 116.8 jit_solution(97980960537834884)
XLA Ops:
  0.6 0.8 add_reduce_fusion
  1.5 0.8 select_reduce_fusion.source_ref
  2.3 110.0 %shard_map.112 = (f32[256,768]{1,0:T(8,128)}, f32[256,768]{1,0:T(8,128)}, f32[256,768]{1,0:T(8,128)}) custom-call(f32[3,256,256]{2,1,0:T(8,128)} %depth_hbm.1, f32[3,256,256]{2,1,0:T(8,128)} %fx_hbm.1, f32[3,256,256]{2,1,0:T(8,128)} %fy_hbm.1, bf16[3,256,256]{2,1,0:T(8,128)(2,1)} %floor_hbm.1, bf16[3,256,256]{2,1,0:T(8,128)(2,1)} %width_hbm.1, ...), custom_call_target="tpu_custom_call" | custom-call | tf_op jit(solution)/shard_map/pallas_call | solution.py:502
  112.3 0.0 copy-start.1
  112.3 2.1 %copy.15 = f32[256,768]{1,0:T(8,128)} copy(f32[256,768]{1,0:T(8,128)} %get-tuple-element.8) | data formatting | bytes 1572864
  114.5 0.0 copy-done.1
  114.5 0.0 copy-start
  114.5 0.9 copy.16
  115.3 0.5 copy-done
  115.9 0.9 copy.17
  (1 shorter events, 0.0 us)
Async XLA Ops:
  112.3 2.1 %copy-start.1 = (f32[256,768]{1,0:T(8,128)S(1)}, f32[256,768]{1,0:T(8,128)}, u32[]{:S(2)}) copy-start(f32[256,768]{1,0:T(8,128)} %get-tuple-element.9) | copy-start | bytes 2359300
  114.5 1.4 %copy-start = (f32[256,768]{1,0:T(8,128)S(1)}, f32[256,768]{1,0:T(8,128)}, u32[]{:S(2)}) copy-start(f32[256,768]{1,0:T(8,128)} %get-tuple-element.10) | copy-start | bytes 2359300

commit v4 on v3

--- a/solution.py
+++ b/solution.py
@@ -27,8 +27,6 @@
 HIGH = 72
 STRIPS = -(-(TILE + 2 * PAD) // HIGH)
 ROWS = STRIPS * HIGH
-EDGE = 1
-SAFE = (TILE + PAD - 1) // HIGH
 COLS = SLOTS * TILE
 WIDE = COLS + LANES
 REACH = 4
@@ -36,6 +34,8 @@
 BLOCKS = WIDE // LANES
 PARTS = 4
 TALL = 64
+FACE_HIGH = 32
+PAIRS = (FIELDS + 1) // 2
 LOG2_E = 1.4426950408889634
 WATER, FLOW_X, FLOW_Y, BED, WIDTH, CHAN, ROUGH = range(FIELDS)
 F32 = jnp.float32
@@ -79,7 +79,7 @@
     depth_ref, fx_ref, fy_ref, floor_ref, width_ref, chan_ref, rough_ref,
     water_out, fx_out, fy_out,
     coded, first_a, first_b, middle, second_a, second_b, arrived,
-    fields, sent_w, sent_e, got_e, got_w, level, volume, cap, inverse, flow_x, flow_y,
+    fields, sent_w, sent_e, got_e, got_w, sent_n, sent_s, got_n, got_s, level, volume, cap, inverse, flow_x, flow_y,
     bed_x, part_x, deep_x, drag_x, gate_x, bed_y, part_y, deep_y, drag_y, gate_y,
     send_sem, recv_sem, local_sem, rim_send, rim_recv, in_sem, out_sem,
 ):
@@ -95,6 +95,8 @@
     east = (row, (col + 1) % NC)
     north = ((row + NX * NZ - 1) % (NX * NZ), col)
     south = ((row + 1) % (NX * NZ), col)
+
+    corners = [(north[0], west[1]), (north[0], east[1]), (south[0], west[1]), (south[0], east[1])]
 
     loads = []
     for slot in range(SLOTS):
@@ -114,7 +116,7 @@
     greeted = [place((own_x + d) % NX, own_z, col) for d in (1, 2, 3)]
     greeted += [place(own_x, (own_z + d) % NZ, col) for d in (1, 2, 3)]
     greeted += [place(own_x, own_z, (col + d) % NC) for d in range(1, NC)]
-    greeted += [north, south]
+    greeted += [north, south] + corners
     for device in greeted:
         pl.semaphore_signal(barrier, inc=1, device_id=device, device_id_type=pl.DeviceIdType.MESH)
 
@@ -257,9 +259,30 @@
         landed(flying[chunk])
         decode(chunk)
 
-    lane = lax.broadcasted_iota(jnp.int32, (TALL, LANES), 1)
+    def rim(number, source, target, device):
+        copy = pltpu.make_async_remote_copy(
+            src_ref=source, dst_ref=target, send_sem=rim_send.at[number],
+            recv_sem=rim_recv.at[number], device_id=device,
+            device_id_type=pl.DeviceIdType.MESH,
+        )
+        copy.start()
+        started.append(copy)
+        return copy
+
+    inner = pl.ds(0, COLS)
+    outer = pl.ds(COLS, LANES)
+    upper = lax.broadcasted_iota(jnp.int32, (PAD, COLS), 0) < REACH
+    top_rows, bottom_rows = pl.ds(PAD, PAD), pl.ds(TILE, PAD)
+    for pair in range(PAIRS):
+        f, g = 2 * pair, min(2 * pair + 1, FIELDS - 1)
+        turned = pltpu.roll(fields[g, top_rows, inner], REACH, 0)
+        sent_n[pair] = jnp.where(upper, fields[f, top_rows, inner], turned)
+        turned = pltpu.roll(fields[g, bottom_rows, inner], REACH, 0)
+        sent_s[pair] = jnp.where(upper, turned, fields[f, bottom_rows, inner])
+    ends = [rim(2, sent_n, got_s, north), rim(3, sent_s, got_n, south)]
 
     def pack(k, _):
+        lane = lax.broadcasted_iota(jnp.int32, (TALL, LANES), 1)
         rows = pl.ds(pl.multiple_of(PAD + k * TALL, 8), TALL)
         left = jnp.zeros((TALL, LANES), F32)
         right = jnp.zeros((TALL, LANES), F32)
@@ -275,23 +298,15 @@
         return 0
 
     lax.fori_loop(0, TILE // TALL, pack, 0)
-
-    def rim(number, source, target, device):
-        copy = pltpu.make_async_remote_copy(
-            src_ref=source, dst_ref=target, send_sem=rim_send.at[number],
-            recv_sem=rim_recv.at[number], device_id=device,
-            device_id_type=pl.DeviceIdType.MESH,
-        )
-        copy.start()
-        started.append(copy)
-        return copy
-
-    side = [rim(0, sent_w, got_e, west), rim(1, sent_e, got_w, east)]
-    inner = pl.ds(0, COLS)
-    outer = pl.ds(COLS, LANES)
-    ends = [
-        rim(2, fields.at[:, pl.ds(PAD, 8), inner], fields.at[:, pl.ds(PAD + TILE, 8), inner], north),
-        rim(3, fields.at[:, pl.ds(TILE, 8), inner], fields.at[:, pl.ds(0, 8), inner], south),
+    middle_rows, early, late = pl.ds(PAD, TILE), pl.ds(0, PAD), pl.ds(PAD + TILE, PAD)
+    final_rows = pl.ds(TILE - PAD, PAD)
+    side = [
+        rim(0, sent_w, got_e.at[middle_rows], west),
+        rim(1, sent_e, got_w.at[middle_rows], east),
+        rim(4, sent_w.at[early], got_e.at[late], corners[0]),
+        rim(5, sent_e.at[early], got_w.at[late], corners[1]),
+        rim(6, sent_w.at[final_rows], got_e.at[early], corners[2]),
+        rim(7, sent_e.at[final_rows], got_w.at[early], corners[3]),
     ]
 
     row_of = lax.broadcasted_iota(jnp.int32, (8, LANES), 0)
@@ -301,16 +316,17 @@
     right_end = lanes_high == LANES - 1
     left_end = lanes_high == 0
 
-    def strip(k):
-        return pl.ds(pl.multiple_of(k * HIGH, 8), HIGH)
-
-    def below_strip(k):
-        return pl.ds(pl.multiple_of(jnp.minimum((k + 1) * HIGH, ROWS - 8), 8), 8)
+    def strip(k, high=HIGH):
+        return pl.ds(pl.multiple_of(k * high, 8), high)
+
+    def below_strip(k, high=HIGH):
+        return pl.ds(pl.multiple_of(jnp.minimum((k + 1) * high, ROWS - 8), 8), 8)
 
     def from_south(values, after):
-        moved = pltpu.roll(values, HIGH - 1, 0)
-        end = jnp.where(bottom, pltpu.roll(after, 7, 0), moved[HIGH - 8 :])
-        return jnp.concatenate([moved[: HIGH - 8], end], 0) if HIGH > 8 else end
+        high = values.shape[0]
+        moved = pltpu.roll(values, high - 1, 0)
+        end = jnp.where(bottom, pltpu.roll(after, 7, 0), moved[high - 8 :])
+        return jnp.concatenate([moved[: high - 8], end], 0) if high > 8 else end
 
     def from_north(values, before):
         moved = pltpu.roll(values, 1, 0)
@@ -321,8 +337,9 @@
         return pl.ds((c % BLOCKS) * LANES, LANES)
 
     def faces(k, c):
-        here = strip(k)
-        there = below_strip(k)
+        here = strip(k, FACE_HIGH)
+        there = below_strip(k, FACE_HIGH)
+        last_lane = lax.broadcasted_iota(jnp.int32, (FACE_HIGH, LANES), 1) == LANES - 1
         water = fields[WATER, here, block(c)]
         bed, width = fields[BED, here, block(c)], fields[WIDTH, here, block(c)]
         chan, rough = fields[CHAN, here, block(c)], fields[ROUGH, here, block(c)]
@@ -335,7 +352,7 @@
 
         def to_east(f, v):
             after = pltpu.roll(fields[f, here, block(c + 1)], LANES - 1, 1)
-            return jnp.where(right_end, after, pltpu.roll(v, LANES - 1, 1))
+            return jnp.where(last_lane, after, pltpu.roll(v, LANES - 1, 1))
 
         def to_south(f, v):
             return from_south(v, fields[f, there, block(c)])
@@ -362,18 +379,20 @@
 
         lax.fori_loop(start, stop, one, 0)
 
-    many_faces(EDGE, SAFE, range(BLOCKS - 2))
+    many_faces(1, TILE // FACE_HIGH, range(BLOCKS - 2))
 
     for copy in side:
         copy.wait_recv()
     at_east = col == NC - 1
     at_west = col == 0
 
+    half = (TILE + 2 * PAD) // 2
+
     def unpack(k, _):
-        source = pl.ds(pl.multiple_of(k * TALL, 8), TALL)
-        rows = pl.ds(pl.multiple_of(PAD + k * TALL, 8), TALL)
-        from_e = got_e[source, :]
-        from_w = got_w[source, :]
+        lane = lax.broadcasted_iota(jnp.int32, (half, LANES), 1)
+        rows = pl.ds(pl.multiple_of(k * half, 8), half)
+        from_e = got_e[rows, :]
+        from_w = got_w[rows, :]
         for f in range(FIELDS):
             low = pltpu.roll(from_e, LANES - REACH * f, 1) if f else from_e
             high = pltpu.roll(from_w, LANES - REACH * (f + 1), 1)
@@ -385,20 +404,21 @@
             fields[f, rows, outer] = mixed
         return 0
 
-    lax.fori_loop(0, TILE // TALL, unpack, 0)
-    ends += [
-        rim(4, fields.at[:, pl.ds(PAD, 8), outer], fields.at[:, pl.ds(PAD + TILE, 8), outer], north),
-        rim(5, fields.at[:, pl.ds(TILE, 8), outer], fields.at[:, pl.ds(0, 8), outer], south),
-    ]
-    many_faces(EDGE, SAFE, range(BLOCKS - 2, BLOCKS))
+    lax.fori_loop(0, 2, unpack, 0)
+    many_faces(1, TILE // FACE_HIGH, range(BLOCKS - 2, BLOCKS))
     for copy in ends:
         copy.wait_recv()
+    for pair in range(PAIRS):
+        for got, rows in ((got_n, early), (got_s, late)):
+            fields[2 * pair, rows, inner] = got[pair]
+            if 2 * pair + 1 < FIELDS:
+                fields[2 * pair + 1, rows, inner] = pltpu.roll(got[pair], REACH, 0)
     first = fields[ROUGH, pl.ds(0, 8), :]
     fields[ROUGH, pl.ds(0, 8), :] = jnp.where(row == 0, -1.0, first)
     last = fields[ROUGH, pl.ds(PAD + TILE, 8), :]
     fields[ROUGH, pl.ds(PAD + TILE, 8), :] = jnp.where(row == NX * NZ - 1, -1.0, last)
-    many_faces(0, EDGE, range(BLOCKS))
-    many_faces(SAFE, STRIPS, range(BLOCKS))
+    many_faces(0, 1, range(BLOCKS))
+    many_faces(TILE // FACE_HIGH, ROWS // FACE_HIGH, range(BLOCKS))
 
     def face_flow(flow, surface, surface_n, bed_f, part_f, deep_f, drag_f, gate_f):
         crest = jnp.maximum(surface, surface_n) - bed_f
@@ -508,14 +528,16 @@
         + [pltpu.VMEM((ROWS, COLS), F32)] * 3
         + [pieces] * 7
         + [pltpu.VMEM((FIELDS, ROWS, WIDE), F32)]
-        + [edge] * 4
+        + [edge] * 2
+        + [pltpu.VMEM((TILE + 2 * PAD, LANES), F32)] * 2
+        + [pltpu.VMEM((PAIRS, PAD, COLS), F32)] * 4
         + [grid] * 16
         + [
             pltpu.SemaphoreType.DMA((6 * CHUNKS * 8,)),
             pltpu.SemaphoreType.DMA((6 * CHUNKS * 8,)),
             pltpu.SemaphoreType.DMA((6 * CHUNKS,)),
-            pltpu.SemaphoreType.DMA((6,)),
-            pltpu.SemaphoreType.DMA((6,)),
+            pltpu.SemaphoreType.DMA((8,)),
+            pltpu.SemaphoreType.DMA((8,)),
             pltpu.SemaphoreType.DMA((SLOTS * FIELDS,)),
             pltpu.SemaphoreType.DMA((PARTS * 3,)),
         ],

time: 117 us -> 116 us (level)
  no operation moved by 1% of the time
where the time goes in v4:
time: 116 us
  Pallas kernels  109 us (94%)
  local copies, waits for them, and re-layouts  4.44 us (4%)
  other arithmetic  1.65 us (1%)
    pallas_call x1, Pallas kernels, body(): pl.pallas_call(migrate_and_route, out_shape=(out, out, out), in_specs=[wh...  109 us
    unnamed x7, local copies, waits for them, and re-layouts  4.44 us

profile of v4, /device:TPU:1, one launch (start us, length us, event | category | flops | bytes accessed | tf_op | source)
XLA Modules:
  0.0 115.6 jit_solution(2383075658104047083)
XLA Ops:
  0.6 0.8 add_reduce_fusion
  1.5 0.8 select_reduce_fusion.source_ref
  2.3 108.9 %shard_map.112 = (f32[256,768]{1,0:T(8,128)}, f32[256,768]{1,0:T(8,128)}, f32[256,768]{1,0:T(8,128)}) custom-call(f32[3,256,256]{2,1,0:T(8,128)} %depth_hbm.1, f32[3,256,256]{2,1,0:T(8,128)} %fx_hbm.1, f32[3,256,256]{2,1,0:T(8,128)} %fy_hbm.1, bf16[3,256,256]{2,1,0:T(8,128)(2,1)} %floor_hbm.1, bf16[3,256,256]{2,1,0:T(8,128)(2,1)} %width_hbm.1, ...), custom_call_target="tpu_custom_call" | custom-call | tf_op jit(solution)/shard_map/pallas_call | solution.py:522
  111.2 0.0 copy-start.1
  111.2 2.1 %copy.15 = f32[256,768]{1,0:T(8,128)} copy(f32[256,768]{1,0:T(8,128)} %get-tuple-element.8) | data formatting | bytes 1572864
  113.3 0.0 copy-done.1
  113.3 0.0 copy-start
  113.3 0.9 copy.16
  114.2 0.5 copy-done
  114.8 0.9 copy.17
  (1 shorter events, 0.0 us)
Async XLA Ops:
  111.2 2.1 %copy-start.1 = (f32[256,768]{1,0:T(8,128)S(1)}, f32[256,768]{1,0:T(8,128)}, u32[]{:S(2)}) copy-start(f32[256,768]{1,0:T(8,128)} %get-tuple-element.9) | copy-start | bytes 2359300
  113.3 1.4 %copy-start = (f32[256,768]{1,0:T(8,128)S(1)}, f32[256,768]{1,0:T(8,128)}, u32[]{:S(2)}) copy-start(f32[256,768]{1,0:T(8,128)} %get-tuple-element.10) | copy-start | bytes 2359300

commit v5 on v4

--- a/solution.py
+++ b/solution.py
@@ -19,8 +19,8 @@
 TILE = 256
 BLOCK = 16
 LANES = 128
-FIRST = ("yxz", "xzy", "zyx") * 2
-SECOND = ("zxy", "yzx", "xyz") * 2
+FIRST = ("yxz", "xzy", "zyx")
+SECOND = ("zxy", "yzx", "xyz")
 PIECES = (CHUNKS, NX, NZ, NC, BLOCK, LANES)
 
 PAD = 8
@@ -78,7 +78,7 @@
     water_hbm, fx_out_hbm, fy_out_hbm,
     depth_ref, fx_ref, fy_ref, floor_ref, width_ref, chan_ref, rough_ref,
     water_out, fx_out, fy_out,
-    coded, first_a, first_b, middle, second_a, second_b, arrived,
+    coded, first_a, first_b, middle_l, middle_r, second_a, second_b, arrived,
     fields, sent_w, sent_e, got_e, got_w, sent_n, sent_s, got_n, got_s, level, volume, cap, inverse, flow_x, flow_y,
     bed_x, part_x, deep_x, drag_x, gate_x, bed_y, part_y, deep_y, drag_y, gate_y,
     send_sem, recv_sem, local_sem, rim_send, rim_recv, in_sem, out_sem,
@@ -98,20 +98,6 @@
 
     corners = [(north[0], west[1]), (north[0], east[1]), (south[0], west[1]), (south[0], east[1])]
 
-    loads = []
-    for slot in range(SLOTS):
-        pairs = (
-            (depth_hbm, depth_ref), (fx_hbm, fx_ref), (fy_hbm, fy_ref), (floor_hbm, floor_ref),
-            (width_hbm, width_ref), (chan_hbm, chan_ref), (rough_hbm, rough_ref),
-        )
-        group = [
-            pltpu.make_async_copy(hbm.at[slot], ref.at[slot], in_sem.at[slot * FIELDS + n])
-            for n, (hbm, ref) in enumerate(pairs)
-        ]
-        for copy in group:
-            copy.start()
-        loads.append(group)
-
     barrier = pltpu.get_barrier_semaphore()
     greeted = [place((own_x + d) % NX, own_z, col) for d in (1, 2, 3)]
     greeted += [place(own_x, (own_z + d) % NZ, col) for d in (1, 2, 3)]
@@ -120,12 +106,28 @@
     for device in greeted:
         pl.semaphore_signal(barrier, inc=1, device_id=device, device_id_type=pl.DeviceIdType.MESH)
 
+    chunks = [slot * HALVES + half for half in range(HALVES) for slot in range(SLOTS)]
+    pairs = (
+        (depth_hbm, depth_ref), (fx_hbm, fx_ref), (fy_hbm, fy_ref), (floor_hbm, floor_ref),
+        (width_hbm, width_ref), (chan_hbm, chan_ref), (rough_hbm, rough_ref),
+    )
+    loads = {}
+    for chunk in chunks:
+        slot, lanes = chunk // HALVES, pl.ds(chunk % HALVES * LANES, LANES)
+        loads[chunk] = [
+            pltpu.make_async_copy(
+                hbm.at[slot, :, lanes], ref.at[slot, :, lanes], in_sem.at[chunk * FIELDS + n]
+            )
+            for n, (hbm, ref) in enumerate(pairs)
+        ]
+        for copy in loads[chunk]:
+            copy.start()
+
     def encode(chunk):
         slot, half = chunk // HALVES, chunk % HALVES
         lanes = pl.ds(half * LANES, LANES)
-        if half == 0:
-            for copy in loads[slot]:
-                copy.wait()
+        for copy in loads[chunk]:
+            copy.wait()
 
         def block(b, _):
             rows = pl.ds(pl.multiple_of(b * BLOCK, BLOCK), BLOCK)
@@ -171,7 +173,7 @@
 
         lax.fori_loop(0, TILE // BLOCK, block, 0)
 
-    def copies(stage, chunk, axis, source, target):
+    def copies(stage, chunk, axis, source, target, taken, put):
         base = (stage * CHUNKS + chunk) * 8
         remote = []
         if axis == "y":
@@ -190,8 +192,8 @@
         for q, (partner, device) in enumerate(zip(partners, devices)):
             remote.append(
                 pltpu.make_async_remote_copy(
-                    src_ref=part(source, chunk, axis, partner),
-                    dst_ref=part(target, chunk, axis, me),
+                    src_ref=part(source, taken, axis, partner),
+                    dst_ref=part(target, put, axis, me),
                     send_sem=send_sem.at[base + q],
                     recv_sem=recv_sem.at[base + q],
                     device_id=device,
@@ -199,16 +201,17 @@
                 )
             )
         local = pltpu.make_async_copy(
-            part(source, chunk, axis, me),
-            part(target, chunk, axis, me),
+            part(source, taken, axis, me),
+            part(target, put, axis, me),
             local_sem.at[stage * CHUNKS + chunk],
         )
         return remote, local
 
     started = []
 
-    def launch(stage, chunk, axis, source, target):
-        remote, local = copies(stage, chunk, axis, source, target)
+    def launch(stage, chunk, axis, source, target, put=None):
+        put = chunk if put is None else put
+        remote, local = copies(stage, chunk, axis, source, target, chunk, put)
         for copy in remote:
             copy.start()
         local.start()
@@ -221,41 +224,48 @@
             copy.wait_recv()
         local.wait()
 
-    encode(0)
+    middles = (middle_l, middle_r)
+    encode(chunks[0])
     pl.semaphore_wait(barrier, len(greeted))
-    flying = []
-    for chunk in range(CHUNKS):
-        if chunk > 0:
+    flying = {}
+    for chunk in chunks:
+        if chunk != chunks[0]:
             encode(chunk)
-        flying.append(launch(0, chunk, FIRST[chunk][0], coded, first_a))
-    for stage, source, target in ((1, first_a, first_b), (2, first_b, middle)):
-        for chunk in range(CHUNKS):
+        flying[chunk] = launch(0, chunk, FIRST[chunk // HALVES][0], coded, first_a)
+    opening = list(started)
+    started.clear()
+    for chunk in chunks:
+        landed(flying[chunk])
+        flying[chunk] = launch(1, chunk, FIRST[chunk // HALVES][1], first_a, first_b)
+    for chunk in chunks:
+        landed(flying[chunk])
+        flying[chunk] = launch(
+            2, chunk, FIRST[chunk // HALVES][2], first_b, middles[chunk % HALVES], chunk // HALVES
+        )
+    for copy in opening:
+        copy.wait_send()
+    ordered = coded.reshape(CHUNKS * DEVICES, BLOCK, LANES)
+    for half in range(HALVES):
+        group = chunks[half * SLOTS : (half + 1) * SLOTS]
+        held = middles[half].reshape(SLOTS * DEVICES, BLOCK, LANES)
+        for chunk in group:
             landed(flying[chunk])
-            flying[chunk] = launch(stage, chunk, FIRST[chunk][stage], source, target)
-    for chunk in range(CHUNKS):
-        landed(flying[chunk])
-
-    for copy in started:
-        copy.wait_send()
-    started.clear()
-    taken = middle.reshape(CHUNKS * DEVICES, BLOCK, LANES)
-    ordered = coded.reshape(CHUNKS * DEVICES, BLOCK, LANES)
-    for chunk in range(CHUNKS):
-        slot, half = chunk // HALVES, chunk % HALVES
-
-        def move(k, _):
-            for u in range(8):
-                d = k * 8 + u
-                ordered[chunk * DEVICES + d] = taken[source_ref[slot * DEVICES + d] + half * DEVICES]
-            return 0
-
-        lax.fori_loop(0, DEVICES // 8, move, 0)
-        flying[chunk] = launch(3, chunk, SECOND[chunk][0], coded, second_a)
+        for chunk in group:
+            slot = chunk // HALVES
+
+            def move(k, _):
+                for u in range(8):
+                    d = k * 8 + u
+                    ordered[chunk * DEVICES + d] = held[source_ref[slot * DEVICES + d]]
+                return 0
+
+            lax.fori_loop(0, DEVICES // 8, move, 0)
+            flying[chunk] = launch(3, chunk, SECOND[slot][0], coded, second_a)
     for stage, source, target in ((4, second_a, second_b), (5, second_b, arrived)):
-        for chunk in range(CHUNKS):
+        for chunk in chunks:
             landed(flying[chunk])
-            flying[chunk] = launch(stage, chunk, SECOND[chunk][stage - 3], source, target)
-    for chunk in range(CHUNKS):
+            flying[chunk] = launch(stage, chunk, SECOND[chunk // HALVES][stage - 3], source, target)
+    for chunk in chunks:
         landed(flying[chunk])
         decode(chunk)
 
@@ -507,7 +517,7 @@
 def body(depth, flow_x, flow_y, floor, width, chan, rough, route, wet_tiles):
     target = (route[:, 0] * NC + route[:, 1]) * SLOTS + route[:, 2]
     old = jnp.arange(DEVICES * SLOTS, dtype=jnp.int32)
-    where_held = (old % SLOTS) * (HALVES * DEVICES) + old // SLOTS
+    where_held = (old % SLOTS) * DEVICES + old // SLOTS
     slot_major = (old % DEVICES) * SLOTS + old // DEVICES
     source = jnp.sum(
         jnp.where(slot_major[:, None] == target[None, :], where_held[None, :], 0), axis=1
@@ -526,7 +536,9 @@
         out_specs=(whole, whole, whole),
         scratch_shapes=[pltpu.VMEM(a.shape, a.dtype) for a in operands]
         + [pltpu.VMEM((ROWS, COLS), F32)] * 3
-        + [pieces] * 7
+        + [pieces] * 3
+        + [pltpu.VMEM((SLOTS,) + PIECES[1:], jnp.int16)] * 2
+        + [pieces] * 3
         + [pltpu.VMEM((FIELDS, ROWS, WIDE), F32)]
         + [edge] * 2
         + [pltpu.VMEM((TILE + 2 * PAD, LANES), F32)] * 2
@@ -538,7 +550,7 @@
             pltpu.SemaphoreType.DMA((6 * CHUNKS,)),
             pltpu.SemaphoreType.DMA((8,)),
             pltpu.SemaphoreType.DMA((8,)),
-            pltpu.SemaphoreType.DMA((SLOTS * FIELDS,)),
+            pltpu.SemaphoreType.DMA((CHUNKS * FIELDS,)),
             pltpu.SemaphoreType.DMA((PARTS * 3,)),
         ],
         compiler_params=pltpu.CompilerParams(

time: 116 us -> 113 us (0.974)
  Pallas kernels: 109 us -> 106 us
    pallas_call x1, Pallas kernels: 109 us -> 106 us  [body(): pl.pallas_call(migrate_and_route, out_shape=(out, out, out), in_specs=[wh...]
where the time goes in v5:
time: 113 us
  Pallas kernels  106 us (94%)
  local copies, waits for them, and re-layouts  4.44 us (4%)
  other arithmetic  1.65 us (1%)
    pallas_call x1, Pallas kernels, body(): pl.pallas_call(migrate_and_route, out_shape=(out, out, out), in_specs=[wh...  106 us
    unnamed x7, local copies, waits for them, and re-layouts  4.44 us

profile of v5, /device:TPU:1, one launch (start us, length us, event | category | flops | bytes accessed | tf_op | source)
XLA Modules:
  0.0 112.5 jit_solution(16411192220445471031)
XLA Ops:
  0.6 0.8 add_reduce_fusion
  1.5 0.8 select_reduce_fusion.source_ref
  2.3 105.8 %shard_map.112 = (f32[256,768]{1,0:T(8,128)}, f32[256,768]{1,0:T(8,128)}, f32[256,768]{1,0:T(8,128)}) custom-call(f32[3,256,256]{2,1,0:T(8,128)} %depth_hbm.1, f32[3,256,256]{2,1,0:T(8,128)} %fx_hbm.1, f32[3,256,256]{2,1,0:T(8,128)} %fy_hbm.1, bf16[3,256,256]{2,1,0:T(8,128)(2,1)} %floor_hbm.1, bf16[3,256,256]{2,1,0:T(8,128)(2,1)} %width_hbm.1, ...), custom_call_target="tpu_custom_call" | custom-call | tf_op jit(solution)/shard_map/pallas_call | solution.py:532
  108.1 0.0 copy-start.1
  108.1 2.1 %copy.15 = f32[256,768]{1,0:T(8,128)} copy(f32[256,768]{1,0:T(8,128)} %get-tuple-element.8) | data formatting | bytes 1572864
  110.2 0.0 copy-done.1
  110.2 0.0 copy-start
  110.2 0.9 copy.16
  111.1 0.5 copy-done
  111.6 0.9 copy.17
  (1 shorter events, 0.0 us)
Async XLA Ops:
  108.1 2.1 %copy-start.1 = (f32[256,768]{1,0:T(8,128)S(1)}, f32[256,768]{1,0:T(8,128)}, u32[]{:S(2)}) copy-start(f32[256,768]{1,0:T(8,128)} %get-tuple-element.9) | copy-start | bytes 2359300
  110.2 1.4 %copy-start = (f32[256,768]{1,0:T(8,128)S(1)}, f32[256,768]{1,0:T(8,128)}, u32[]{:S(2)}) copy-start(f32[256,768]{1,0:T(8,128)} %get-tuple-element.10) | copy-start | bytes 2359300

commit v6 on v5

--- a/solution.py
+++ b/solution.py
@@ -34,6 +34,7 @@
 BLOCKS = WIDE // LANES
 PARTS = 4
 TALL = 64
+FOLD = 32
 FACE_HIGH = 32
 PAIRS = (FIELDS + 1) // 2
 LOG2_E = 1.4426950408889634
@@ -74,14 +75,15 @@
 
 
 def migrate_and_route(
-    depth_hbm, fx_hbm, fy_hbm, floor_hbm, width_hbm, chan_hbm, rough_hbm, source_ref, wet_ref,
+    depth_hbm, fx_hbm, fy_hbm, floor_hbm, width_hbm, chan_hbm, rough_hbm, route_ref, wet_ref,
     water_hbm, fx_out_hbm, fy_out_hbm,
     depth_ref, fx_ref, fy_ref, floor_ref, width_ref, chan_ref, rough_ref,
     water_out, fx_out, fy_out,
     coded, first_a, first_b, middle_l, middle_r, second_a, second_b, arrived,
     fields, sent_w, sent_e, got_e, got_w, sent_n, sent_s, got_n, got_s, level, volume, cap, inverse, flow_x, flow_y,
     bed_x, part_x, deep_x, drag_x, gate_x, bed_y, part_y, deep_y, drag_y, gate_y,
-    send_sem, recv_sem, local_sem, rim_send, rim_recv, in_sem, out_sem,
+    source_rows, source_ref, send_sem, recv_sem, local_sem, rim_send, rim_recv, in_sem, out_sem,
+    source_sem,
 ):
     row = lax.axis_index("row")
     col = lax.axis_index("col")
@@ -232,6 +234,20 @@
         if chunk != chunks[0]:
             encode(chunk)
         flying[chunk] = launch(0, chunk, FIRST[chunk // HALVES][0], coded, first_a)
+    route = route_ref[...]
+    target = (route[0:1] * NC + route[1:2]) * SLOTS + route[2:3]
+    target = jnp.transpose(jnp.broadcast_to(target, (8, SLOTS * DEVICES)))[:, 0:1]
+    old = lax.broadcasted_iota(jnp.int32, (SLOTS * DEVICES, LANES), 0)
+    new = lax.broadcasted_iota(jnp.int32, (SLOTS * DEVICES, LANES), 1) * SLOTS
+    device = jnp.right_shift(old * 171, 9)
+    where_held = (old - device * SLOTS) * DEVICES + device
+    source_rows[...] = jnp.zeros_like(source_rows)
+    for slot in range(SLOTS):
+        found = jnp.sum(jnp.where(new + slot == target, where_held, 0), axis=0, keepdims=True)
+        source_rows[slot : slot + 1, :] = jnp.minimum(found, SLOTS * DEVICES - 1)
+    to_scalars = pltpu.make_async_copy(source_rows, source_ref, source_sem)
+    to_scalars.start()
+    to_scalars.wait()
     opening = list(started)
     started.clear()
     for chunk in chunks:
@@ -256,7 +272,7 @@
             def move(k, _):
                 for u in range(8):
                     d = k * 8 + u
-                    ordered[chunk * DEVICES + d] = held[source_ref[slot * DEVICES + d]]
+                    ordered[chunk * DEVICES + d] = held[source_ref[slot, d]]
                 return 0
 
             lax.fori_loop(0, DEVICES // 8, move, 0)
@@ -291,32 +307,29 @@
         sent_s[pair] = jnp.where(upper, turned, fields[f, bottom_rows, inner])
     ends = [rim(2, sent_n, got_s, north), rim(3, sent_s, got_n, south)]
 
-    def pack(k, _):
-        lane = lax.broadcasted_iota(jnp.int32, (TALL, LANES), 1)
-        rows = pl.ds(pl.multiple_of(PAD + k * TALL, 8), TALL)
-        left = jnp.zeros((TALL, LANES), F32)
-        right = jnp.zeros((TALL, LANES), F32)
+    lane = lax.broadcasted_iota(jnp.int32, (TALL, LANES), 1)
+    left = jnp.zeros((TALL, LANES), F32)
+    right = jnp.zeros((TALL, LANES), F32)
+    for k in range(TILE // TALL):
+        rows = pl.ds(PAD + k * TALL, TALL)
         for f in range(FIELDS):
-            here = (lane >= REACH * f) & (lane < REACH * (f + 1))
+            start = FOLD * k + REACH * f
+            here = (lane >= start) & (lane < start + REACH)
             low = fields[f, rows, pl.ds(0, LANES)]
             high = fields[f, rows, pl.ds(COLS - LANES, LANES)]
-            left = jnp.where(here, pltpu.roll(low, REACH * f, 1) if f else low, left)
-            right = jnp.where(here, pltpu.roll(high, REACH * (f + 1), 1), right)
-        out = pl.ds(pl.multiple_of(k * TALL, 8), TALL)
-        sent_w[out, :] = left
-        sent_e[out, :] = right
-        return 0
-
-    lax.fori_loop(0, TILE // TALL, pack, 0)
-    middle_rows, early, late = pl.ds(PAD, TILE), pl.ds(0, PAD), pl.ds(PAD + TILE, PAD)
-    final_rows = pl.ds(TILE - PAD, PAD)
+            left = jnp.where(here, pltpu.roll(low, start, 1) if start else low, left)
+            right = jnp.where(here, pltpu.roll(high, start + REACH, 1), right)
+    sent_w[...] = left
+    sent_e[...] = right
+    early, late = pl.ds(0, PAD), pl.ds(PAD + TILE, PAD)
+    middle_rows, last_rows, next_rows = pl.ds(PAD, TALL), pl.ds(TALL - PAD, PAD), pl.ds(PAD + TALL, PAD)
     side = [
         rim(0, sent_w, got_e.at[middle_rows], west),
         rim(1, sent_e, got_w.at[middle_rows], east),
-        rim(4, sent_w.at[early], got_e.at[late], corners[0]),
-        rim(5, sent_e.at[early], got_w.at[late], corners[1]),
-        rim(6, sent_w.at[final_rows], got_e.at[early], corners[2]),
-        rim(7, sent_e.at[final_rows], got_w.at[early], corners[3]),
+        rim(4, sent_w.at[early], got_e.at[next_rows], corners[0]),
+        rim(5, sent_e.at[early], got_w.at[next_rows], corners[1]),
+        rim(6, sent_w.at[last_rows], got_e.at[early], corners[2]),
+        rim(7, sent_e.at[last_rows], got_w.at[early], corners[3]),
     ]
 
     row_of = lax.broadcasted_iota(jnp.int32, (8, LANES), 0)
@@ -354,11 +367,11 @@
         bed, width = fields[BED, here, block(c)], fields[WIDTH, here, block(c)]
         chan, rough = fields[CHAN, here, block(c)], fields[ROUGH, here, block(c)]
         level[here, block(c)] = bed + water
-        volume[here, block(c)] = CELL * width * jnp.minimum(water, chan) + CELL * CELL * (
-            jnp.maximum(water - chan, 0.0)
-        )
-        cap[here, block(c)] = CELL * width * chan
-        inverse[here, block(c)] = 1.0 / (CELL * width) - 1.0 / (CELL * CELL)
+        volume[here, block(c)] = (CELL / STEP) * width * jnp.minimum(water, chan) + (
+            CELL * CELL / STEP
+        ) * jnp.maximum(water - chan, 0.0)
+        cap[here, block(c)] = (CELL / STEP) * width * chan
+        inverse[here, block(c)] = (STEP / CELL) / width - STEP / (CELL * CELL)
 
         def to_east(f, v):
             after = pltpu.roll(fields[f, here, block(c + 1)], LANES - 1, 1)
@@ -396,25 +409,22 @@
     at_east = col == NC - 1
     at_west = col == 0
 
-    half = (TILE + 2 * PAD) // 2
-
-    def unpack(k, _):
-        lane = lax.broadcasted_iota(jnp.int32, (half, LANES), 1)
-        rows = pl.ds(pl.multiple_of(k * half, 8), half)
-        from_e = got_e[rows, :]
-        from_w = got_w[rows, :]
+    segments = [(early, early, FOLD * (TILE // TALL - 1)), (late, next_rows, 0)]
+    segments += [(pl.ds(PAD + k * TALL, TALL), middle_rows, FOLD * k) for k in range(TILE // TALL)]
+    for rows, got, fold in segments:
+        from_e, from_w = got_e[got, :], got_w[got, :]
+        at = lax.broadcasted_iota(jnp.int32, from_e.shape, 1)
         for f in range(FIELDS):
-            low = pltpu.roll(from_e, LANES - REACH * f, 1) if f else from_e
-            high = pltpu.roll(from_w, LANES - REACH * (f + 1), 1)
+            start = fold + REACH * f
+            low = pltpu.roll(from_e, LANES - start, 1) if start else from_e
+            high = pltpu.roll(from_w, LANES - REACH - start, 1) if start < LANES - REACH else from_w
             if f == ROUGH:
                 low = jnp.where(at_east, -1.0, low)
                 high = jnp.where(at_west, -1.0, high)
             fill = 1.0 if f in (WIDTH, CHAN) else (-1.0 if f == ROUGH else 0.0)
-            mixed = jnp.where(lane < REACH, low, jnp.where(lane >= LANES - REACH, high, fill))
+            mixed = jnp.where(at < REACH, low, jnp.where(at >= LANES - REACH, high, fill))
             fields[f, rows, outer] = mixed
-        return 0
-
-    lax.fori_loop(0, 2, unpack, 0)
+
     many_faces(1, TILE // FACE_HIGH, range(BLOCKS - 2, BLOCKS))
     for copy in ends:
         copy.wait_recv()
@@ -471,9 +481,9 @@
                 sunk.append(end)
                 from_w = jnp.where(left_end, passed[c - 1], passed[c])
                 inflow = from_w - new_x[c] + from_n - new_y
-                held = jnp.maximum(volume[here, b] + STEP * inflow, 0.0)
+                held = jnp.maximum(volume[here, b] + inflow, 0.0)
                 water = jnp.minimum(held, cap[here, b]) * inverse[here, b] + held * (
-                    1.0 / (CELL * CELL)
+                    STEP / (CELL * CELL)
                 )
                 if not final:
                     flow_x[here, b] = new_x[c]
@@ -515,24 +525,17 @@
 
 
 def body(depth, flow_x, flow_y, floor, width, chan, rough, route, wet_tiles):
-    target = (route[:, 0] * NC + route[:, 1]) * SLOTS + route[:, 2]
-    old = jnp.arange(DEVICES * SLOTS, dtype=jnp.int32)
-    where_held = (old % SLOTS) * DEVICES + old // SLOTS
-    slot_major = (old % DEVICES) * SLOTS + old // DEVICES
-    source = jnp.sum(
-        jnp.where(slot_major[:, None] == target[None, :], where_held[None, :], 0), axis=1
-    )
     whole = pl.BlockSpec(memory_space=pl.ANY)
     smem = pl.BlockSpec(memory_space=pltpu.SMEM)
     pieces = pltpu.VMEM(PIECES, jnp.int16)
     grid = pltpu.VMEM((ROWS, WIDE), F32)
-    edge = pltpu.VMEM((TILE, LANES), F32)
+    edge = pltpu.VMEM((TALL, LANES), F32)
     out = jax.ShapeDtypeStruct((TILE, COLS), F32)
     operands = (depth, flow_x, flow_y, floor, width, chan, rough)
     return pl.pallas_call(
         migrate_and_route,
         out_shape=(out, out, out),
-        in_specs=[whole] * 7 + [smem] * 2,
+        in_specs=[whole] * 7 + [pl.BlockSpec(memory_space=pltpu.VMEM), smem],
         out_specs=(whole, whole, whole),
         scratch_shapes=[pltpu.VMEM(a.shape, a.dtype) for a in operands]
         + [pltpu.VMEM((ROWS, COLS), F32)] * 3
@@ -541,9 +544,10 @@
         + [pieces] * 3
         + [pltpu.VMEM((FIELDS, ROWS, WIDE), F32)]
         + [edge] * 2
-        + [pltpu.VMEM((TILE + 2 * PAD, LANES), F32)] * 2
+        + [pltpu.VMEM((TALL + 2 * PAD, LANES), F32)] * 2
         + [pltpu.VMEM((PAIRS, PAD, COLS), F32)] * 4
         + [grid] * 16
+        + [pltpu.VMEM((8, LANES), jnp.int32), pltpu.SMEM((8, LANES), jnp.int32)]
         + [
             pltpu.SemaphoreType.DMA((6 * CHUNKS * 8,)),
             pltpu.SemaphoreType.DMA((6 * CHUNKS * 8,)),
@@ -552,11 +556,12 @@
             pltpu.SemaphoreType.DMA((8,)),
             pltpu.SemaphoreType.DMA((CHUNKS * FIELDS,)),
             pltpu.SemaphoreType.DMA((PARTS * 3,)),
+            pltpu.SemaphoreType.DMA,
         ],
         compiler_params=pltpu.CompilerParams(
             collective_id=0, has_side_effects=True, vmem_limit_bytes=58 * 2**20
         ),
-    )(*operands, source, wet_tiles)
+    )(*operands, route.T, wet_tiles)
 
 
 def solution(mesh):

time: 113 us -> 111 us (0.982)
  other arithmetic: 1.65 us -> 0 us
where the time goes in v6:
time: 111 us
  Pallas kernels  106 us (95%)
  local copies, waits for them, and re-layouts  4.44 us (4%)
    pallas_call x1, Pallas kernels, body(): pl.pallas_call(migrate_and_route, out_shape=(out, out, out), in_specs=[wh...  106 us
    unnamed x7, local copies, waits for them, and re-layouts  4.44 us

profile of v6, /device:TPU:1, one launch (start us, length us, event | category | flops | bytes accessed | tf_op | source)
XLA Modules:
  0.0 110.9 jit_solution(15525897682360509102)
XLA Ops:
  0.6 105.8 %shard_map.112 = (f32[256,768]{1,0:T(8,128)}, f32[256,768]{1,0:T(8,128)}, f32[256,768]{1,0:T(8,128)}) custom-call(f32[3,256,256]{2,1,0:T(8,128)} %depth_hbm.1, f32[3,256,256]{2,1,0:T(8,128)} %fx_hbm.1, f32[3,256,256]{2,1,0:T(8,128)} %fy_hbm.1, bf16[3,256,256]{2,1,0:T(8,128)(2,1)} %floor_hbm.1, bf16[3,256,256]{2,1,0:T(8,128)(2,1)} %width_hbm.1, ...), custom_call_target="tpu_custom_call" | custom-call | tf_op jit(solution)/shard_map/pallas_call | solution.py:535
  106.5 0.0 copy-start.1
  106.5 2.1 %copy.15 = f32[256,768]{1,0:T(8,128)} copy(f32[256,768]{1,0:T(8,128)} %get-tuple-element.6) | data formatting | bytes 1572864
  108.6 0.0 copy-done.1
  108.6 0.0 copy-start
  108.6 0.9 copy.16
  109.5 0.5 copy-done
  110.0 0.9 copy.17
Async XLA Ops:
  106.5 2.1 %copy-start.1 = (f32[256,768]{1,0:T(8,128)S(1)}, f32[256,768]{1,0:T(8,128)}, u32[]{:S(2)}) copy-start(f32[256,768]{1,0:T(8,128)} %get-tuple-element.7) | copy-start | bytes 2359300
  108.6 1.4 %copy-start = (f32[256,768]{1,0:T(8,128)S(1)}, f32[256,768]{1,0:T(8,128)}, u32[]{:S(2)}) copy-start(f32[256,768]{1,0:T(8,128)} %get-tuple-element.8) | copy-start | bytes 2359300

commit v7 on v6

--- a/solution.py
+++ b/solution.py
@@ -24,7 +24,7 @@
 PIECES = (CHUNKS, NX, NZ, NC, BLOCK, LANES)
 
 PAD = 8
-HIGH = 72
+HIGH = 96
 STRIPS = -(-(TILE + 2 * PAD) // HIGH)
 ROWS = STRIPS * HIGH
 COLS = SLOTS * TILE
@@ -32,7 +32,7 @@
 REACH = 4
 FIELDS = 7
 BLOCKS = WIDE // LANES
-PARTS = 4
+PARTS = 2
 TALL = 64
 FOLD = 32
 FACE_HIGH = 32
@@ -150,7 +150,7 @@
             put(7, to_code(rough_ref[slot, rows, lanes].astype(F32) * 8192.0))
             return 0
 
-        lax.fori_loop(0, TILE // BLOCK, block, 0)
+        lax.fori_loop(0, TILE // BLOCK, block, 0, unroll=2)
 
     def decode(chunk):
         slot, half = chunk // HALVES, chunk % HALVES
@@ -173,7 +173,7 @@
             fields[ROUGH, rows, lanes] = get(7) * (1.0 / 8192.0) * wet - (1.0 - wet)
             return 0
 
-        lax.fori_loop(0, TILE // BLOCK, block, 0)
+        lax.fori_loop(0, TILE // BLOCK, block, 0, unroll=4)
 
     def copies(stage, chunk, axis, source, target, taken, put):
         base = (stage * CHUNKS + chunk) * 8

time: 111 us -> 110 us (level)
  no operation moved by 1% of the time
where the time goes in v7:
time: 110 us
  Pallas kernels  105 us (95%)
  local copies, waits for them, and re-layouts  4.44 us (4%)
    pallas_call x1, Pallas kernels, body(): pl.pallas_call(migrate_and_route, out_shape=(out, out, out), in_specs=[wh...  105 us
    unnamed x7, local copies, waits for them, and re-layouts  4.44 us

profile of v7, /device:TPU:1, one launch (start us, length us, event | category | flops | bytes accessed | tf_op | source)
XLA Modules:
  0.0 110.0 jit_solution(11352834363808021398)
XLA Ops:
  0.6 104.9 %shard_map.112 = (f32[256,768]{1,0:T(8,128)}, f32[256,768]{1,0:T(8,128)}, f32[256,768]{1,0:T(8,128)}) custom-call(f32[3,256,256]{2,1,0:T(8,128)} %depth_hbm.1, f32[3,256,256]{2,1,0:T(8,128)} %fx_hbm.1, f32[3,256,256]{2,1,0:T(8,128)} %fy_hbm.1, bf16[3,256,256]{2,1,0:T(8,128)(2,1)} %floor_hbm.1, bf16[3,256,256]{2,1,0:T(8,128)(2,1)} %width_hbm.1, ...), custom_call_target="tpu_custom_call" | custom-call | tf_op jit(solution)/shard_map/pallas_call | solution.py:535
  105.5 0.0 copy-start.1
  105.5 2.1 %copy.15 = f32[256,768]{1,0:T(8,128)} copy(f32[256,768]{1,0:T(8,128)} %get-tuple-element.6) | data formatting | bytes 1572864
  107.7 0.0 copy-done.1
  107.7 0.0 copy-start
  107.7 0.9 copy.16
  108.6 0.5 copy-done
  109.1 0.9 copy.17
Async XLA Ops:
  105.5 2.1 %copy-start.1 = (f32[256,768]{1,0:T(8,128)S(1)}, f32[256,768]{1,0:T(8,128)}, u32[]{:S(2)}) copy-start(f32[256,768]{1,0:T(8,128)} %get-tuple-element.7) | copy-start | bytes 2359300
  107.7 1.4 %copy-start = (f32[256,768]{1,0:T(8,128)S(1)}, f32[256,768]{1,0:T(8,128)}, u32[]{:S(2)}) copy-start(f32[256,768]{1,0:T(8,128)} %get-tuple-element.8) | copy-start | bytes 2359300

commit v8 on v7

--- a/solution.py
+++ b/solution.py
@@ -297,16 +297,6 @@
 
     inner = pl.ds(0, COLS)
     outer = pl.ds(COLS, LANES)
-    upper = lax.broadcasted_iota(jnp.int32, (PAD, COLS), 0) < REACH
-    top_rows, bottom_rows = pl.ds(PAD, PAD), pl.ds(TILE, PAD)
-    for pair in range(PAIRS):
-        f, g = 2 * pair, min(2 * pair + 1, FIELDS - 1)
-        turned = pltpu.roll(fields[g, top_rows, inner], REACH, 0)
-        sent_n[pair] = jnp.where(upper, fields[f, top_rows, inner], turned)
-        turned = pltpu.roll(fields[g, bottom_rows, inner], REACH, 0)
-        sent_s[pair] = jnp.where(upper, turned, fields[f, bottom_rows, inner])
-    ends = [rim(2, sent_n, got_s, north), rim(3, sent_s, got_n, south)]
-
     lane = lax.broadcasted_iota(jnp.int32, (TALL, LANES), 1)
     left = jnp.zeros((TALL, LANES), F32)
     right = jnp.zeros((TALL, LANES), F32)
@@ -331,6 +321,15 @@
         rim(6, sent_w.at[last_rows], got_e.at[early], corners[2]),
         rim(7, sent_e.at[last_rows], got_w.at[early], corners[3]),
     ]
+    upper = lax.broadcasted_iota(jnp.int32, (PAD, COLS), 0) < REACH
+    top_rows, bottom_rows = pl.ds(PAD, PAD), pl.ds(TILE, PAD)
+    for pair in range(PAIRS):
+        f, g = 2 * pair, min(2 * pair + 1, FIELDS - 1)
+        turned = pltpu.roll(fields[g, top_rows, inner], REACH, 0)
+        sent_n[pair] = jnp.where(upper, fields[f, top_rows, inner], turned)
+        turned = pltpu.roll(fields[g, bottom_rows, inner], REACH, 0)
+        sent_s[pair] = jnp.where(upper, turned, fields[f, bottom_rows, inner])
+    ends = [rim(2, sent_n, got_s, north), rim(3, sent_s, got_n, south)]
 
     row_of = lax.broadcasted_iota(jnp.int32, (8, LANES), 0)
     bottom = row_of == 7

time: 110 us -> 109 us (level)
  no operation moved by 1% of the time
where the time goes in v8:
time: 109 us
  Pallas kernels  104 us (95%)
  local copies, waits for them, and re-layouts  4.44 us (4%)
    pallas_call x1, Pallas kernels, body(): pl.pallas_call(migrate_and_route, out_shape=(out, out, out), in_specs=[wh...  104 us
    unnamed x7, local copies, waits for them, and re-layouts  4.44 us

profile of v8, /device:TPU:1, one launch (start us, length us, event | category | flops | bytes accessed | tf_op | source)
XLA Modules:
  0.0 109.0 jit_solution(4953398220182061261)
XLA Ops:
  0.6 103.9 %shard_map.112 = (f32[256,768]{1,0:T(8,128)}, f32[256,768]{1,0:T(8,128)}, f32[256,768]{1,0:T(8,128)}) custom-call(f32[3,256,256]{2,1,0:T(8,128)} %depth_hbm.1, f32[3,256,256]{2,1,0:T(8,128)} %fx_hbm.1, f32[3,256,256]{2,1,0:T(8,128)} %fy_hbm.1, bf16[3,256,256]{2,1,0:T(8,128)(2,1)} %floor_hbm.1, bf16[3,256,256]{2,1,0:T(8,128)(2,1)} %width_hbm.1, ...), custom_call_target="tpu_custom_call" | custom-call | tf_op jit(solution)/shard_map/pallas_call | solution.py:534
  104.5 0.0 copy-start.1
  104.5 2.1 %copy.15 = f32[256,768]{1,0:T(8,128)} copy(f32[256,768]{1,0:T(8,128)} %get-tuple-element.6) | data formatting | bytes 1572864
  106.7 0.0 copy-done.1
  106.7 0.0 copy-start
  106.7 0.9 copy.16
  107.6 0.5 copy-done
  108.1 0.9 copy.17
Async XLA Ops:
  104.5 2.1 %copy-start.1 = (f32[256,768]{1,0:T(8,128)S(1)}, f32[256,768]{1,0:T(8,128)}, u32[]{:S(2)}) copy-start(f32[256,768]{1,0:T(8,128)} %get-tuple-element.7) | copy-start | bytes 2359300
  106.7 1.4 %copy-start = (f32[256,768]{1,0:T(8,128)S(1)}, f32[256,768]{1,0:T(8,128)}, u32[]{:S(2)}) copy-start(f32[256,768]{1,0:T(8,128)} %get-tuple-element.8) | copy-start | bytes 2359300
